TPU v7x, 512 devices: a whole 4x4x16 slice. The times are simulated.
512 devices in a mesh: dp: 32 (over y, x, core), mp: 16 (over z).
Axes of the slice: x: 4, y: 4, z: 16, core: 2. Of those that a mesh axis runs over, the one named last changes fastest.
Arguments:
- replica_grads: bfloat16 [32, 4096, 2048], P('dp', None, 'mp'), may hold values from -64 to 64, as said below
- weights: float32 [4096, 2048], P('dp', 'mp'), may hold values from -0.00390625 to 0.00390625
- row_state: float32 [4096], P('dp'), may hold values from 0.02 to 0.5
- col_state: float32 [2048], P('mp'), may hold values from 0.02 to 0.5
Outputs:
- new_weights: float32 [4096, 2048], P(None, 'mp')
- update: float32 [4096, 2048], P('dp', 'mp')
- new_row_state: float32 [4096], P('dp')
- new_col_state: float32 [2048], P('mp')
- rms_value: float32 [], replicated
Inputs may be any that keep to these rules, and one draw needn't show every extreme that they name: `replica_grads`: gradient entries have row and column scales that differ over the matrix.
All inputs are finite; a program needn't handle non-finite values.
Results may differ from a plain program's by a relative error of at most 0.0003.
Values sent between devices are 32-bit elements; how exact they have to be, the bound alone decides.
No kernel may reach another device: no remote copies, remote signals or barrier semaphores. Data moves between devices by JAX's collectives and lax.ppermute only.
A program may use at most 64 MiB of HBM per device.

v0:
```python
import jax
import jax.numpy as jnp
from jax import lax
from jax.sharding import PartitionSpec as P

D = 4096
STEP = 10
FLAT = 2048


def per_device(replica_grads, weights, row_state, col_state):
    decay_rate = 1.0 - float(STEP) ** (-0.8)
    own_grad = replica_grads[0].astype(jnp.float32)
    mean_grad = lax.psum_scatter(own_grad, "dp", scatter_dimension=0, tiled=True) / float(
        lax.axis_size("dp")
    )
    square = mean_grad * mean_grad + 1e-30
    col_part = jnp.sum(square, 0)
    row_sums = lax.psum(jnp.sum(square, 1), "mp")
    row_new = decay_rate * row_state + (1.0 - decay_rate) * (row_sums / FLAT)
    col_sums = lax.psum(col_part, "dp")
    row_summed = lax.psum(jnp.sum(row_new), "dp")
    col_new = decay_rate * col_state + (1.0 - decay_rate) * (col_sums / D)
    row_mean = row_summed / D
    raw_update = mean_grad / jnp.sqrt(row_new[:, None] * col_new[None, :] / row_mean)
    clip_total = lax.psum(jnp.sum(raw_update * raw_update), ("dp", "mp"))
    rms_value = jnp.sqrt(clip_total / (D * FLAT))
    update = raw_update / jnp.maximum(1.0, rms_value)
    stepped = weights - 0.001 * update
    gathered = lax.all_gather(stepped, "dp", axis=0, tiled=True)
    return (gathered, update, row_new, col_new, rms_value)


def solution(mesh):
    in_specs = (P("dp", None, "mp"), P("dp", "mp"), P("dp"), P("mp"))
    out_specs = (P(None, "mp"), P("dp", "mp"), P("dp"), P("mp"), P())
    return jax.shard_map(
        per_device, mesh=mesh, in_specs=in_specs, out_specs=out_specs, check_vma=False
    )
```

profile of v0, /device:TPU:1, one launch (start us, length us, event | category | flops | bytes accessed | tf_op | source)
XLA Modules:
  0.0 385.2 jit_solution(12890216080313460814)
XLA Ops:
  7.2 0.0 copy-start.3
  7.2 0.0 copy-start.4
  7.2 0.0 copy-start
  7.2 0.0 reduce-scatter.2.cloned.1.call-start
  7.2 2.7 bitcast_convert_fusion
  9.9 0.0 reduce-scatter.2.cloned.1.call-update
  9.9 0.0 all-gather.2.cloned.1.call-start
  10.0 108.7 %reduce-scatter.2.cloned.1.call-done = f32[128,128]{1,0:T(8,128)} async-done(((f32[4096,128]{1,0:T(8,128)}), f32[128,128]{1,0:T(8,128)}) %reduce-scatter.2.cloned.1.call-update) | async-done | bytes 65552 | tf_op jit(solution)/shard_map/reduce_scatter | solution.py:14
  118.7 0.9 fusion
  119.6 24.1 %psum.28 = f32[128]{0:T(128)S(1)} all-reduce(f32[128]{0:T(128)S(1)} %get-tuple-element.6), channel_id=1, replica_groups=mesh['dp'=32,'mp'=16] {'mp'}, use_global_device_ids=true, to_apply=%region_2.0 | all-reduce | flops 128 | bytes 1024 | tf_op jit(solution)/shard_map/psum | solution.py:19
  143.8 0.0 copy-done.3
  143.8 0.6 fusion.2
  144.4 0.0 copy-start.1
  144.4 72.0 %all-reduce = (f32[]{:T(128)}, f32[128]{0:T(128)S(1)}) all-reduce(f32[]{:T(128)} %get-tuple-element.11, f32[128]{0:T(128)S(1)} %get-tuple-element.5), channel_id=1, replica_groups=mesh['dp'=32,'mp'=16] {'dp'}, use_global_device_ids=true, to_apply=%region_6.0 | all-reduce | flops 129 | bytes 1032 | tf_op jit(solution)/shard_map/psum | solution.py:22
  217.1 0.0 copy-done.4
  217.1 0.0 copy-start.2
  217.1 1.5 multiply_reduce_fusion
  218.6 99.5 %psum.31 = f32[]{:T(128)} all-reduce(f32[]{:T(128)} %multiply_reduce_fusion), channel_id=1, replica_groups=mesh['dp'=32,'mp'=16] {'dp','mp'}, use_global_device_ids=true, to_apply=%region_8.0 | all-reduce | flops 1 | bytes 8 | tf_op jit(solution)/shard_map/psum | solution.py:26
  318.9 0.0 copy-done
  318.9 1.6 multiply_subtract_fusion
  320.5 0.0 all-gather.2.cloned.1.call-update
  320.5 53.7 %all-gather.2.cloned.1.call-done = f32[4096,128]{1,0:T(8,128)} async-done(((f32[128,128]{1,0:T(8,128)}), f32[4096,128]{1,0:T(8,128)}) %all-gather.2.cloned.1.call-update) | async-done | bytes 2097168 | tf_op jit(solution)/shard_map/all_gather | solution.py:30
  374.2 3.0 copy.10
  377.3 0.0 copy-done.1
  377.3 0.0 copy-done.2
  (1 shorter events, 0.0 us)
Async XLA Ops:
  7.2 136.6 %copy-start.3 = (f32[128]{0:T(128)S(1)}, f32[128]{0:T(128)}, u32[]{:S(2)}) copy-start(f32[128]{0:T(128)} %param.6) | copy-start | bytes 1540
  7.2 209.9 %copy-start.4 = (f32[128]{0:T(128)S(1)}, f32[128]{0:T(128)}, u32[]{:S(2)}) copy-start(f32[128]{0:T(128)} %param.7) | copy-start | bytes 1540
  7.2 311.7 %copy-start = (f32[128,128]{1,0:T(8,128)S(1)}, f32[128,128]{1,0:T(8,128)}, u32[]{:S(2)}) copy-start(f32[128,128]{1,0:T(8,128)} %param.5) | copy-start | bytes 196612
  7.2 111.5 %reduce-scatter.2.cloned.1.call-start = ((), (), s32[]{:S(2)}) async-start(), calls=%async_computation.1 | async-start | bytes 2162688 | tf_op jit(solution)/shard_map/reduce_scatter | solution.py:14
  9.9 364.3 %all-gather.2.cloned.1.call-start = ((), (), s32[]{:S(2)}) async-start(), calls=%async_computation.2 | async-start | bytes 2162688 | tf_op jit(solution)/shard_map/all_gather | solution.py:30
  144.4 232.9 %copy-start.1 = (f32[128]{0:T(128)}, f32[128]{0:T(128)S(1)}, u32[]{:S(2)}) copy-start(f32[128]{0:T(128)S(1)} %get-tuple-element.20) | copy-start | bytes 1540
  217.1 160.2 %copy-start.2 = (f32[128]{0:T(128)}, f32[128]{0:T(128)S(1)}, u32[]{:S(2)}) copy-start(f32[128]{0:T(128)S(1)} %multiply_add_fusion.1) | copy-start | bytes 1540
Sparse Core Ops, SparseCore 0:
  13.0 105.6 reduce-scatter.1
  320.6 53.5 all-gather.1
where the time goes:
time: 386 us; the launch traced here: 385 us
  blocking collectives  196 us (51%)
  waiting for transfers between devices  162 us (42%)
  between operations  16.6 us (4%)
  other arithmetic  7.37 us (2%)
    reduce_scatter x1, waiting for transfers between devices, per_device(): lax.psum_scatter(own_grad, 'dp', scatter_dimension=0, tiled=True)  109 us
    psum x1, blocking collectives, per_device(): clip_total = lax.psum(jnp.sum(raw_update * raw_update), ('dp', 'mp'))  99.5 us
    psum x1, blocking collectives, per_device(): row_summed = lax.psum(jnp.sum(row_new), 'dp')  72 us
    all_gather x1, waiting for transfers between devices, per_device(): gathered = lax.all_gather(stepped, 'dp', axis=0, tiled=True)  53.7 us
    psum x1, blocking collectives, per_device(): row_sums = lax.psum(jnp.sum(square, 1), 'mp')  24.1 us
  transfers between devices with their start and end apart: 2, of which 2 were waited for; matrix products, arithmetic and copies ran while one was open for 0% of the time, Pallas kernels for 0%

commit v1 on v0

v1 whole, which is shorter than its diff:
```python
import jax
import jax.numpy as jnp
from jax import lax
from jax.sharding import Mesh, PartitionSpec as P

D = 4096
STEP = 10
FLAT = 2048
Q, C, Z = 16, 2, 16
DP = ("q", "c")
SWAP = [(0, 1), (1, 0)]


def share(x, axes, n):
    return lax.all_to_all(
        jnp.broadcast_to(x[None], (n, *x.shape)), axes, 0, 0, tiled=True
    )


def per_device(replica_grads, weights, row_state, col_state):
    decay_rate = 1.0 - float(STEP) ** (-0.8)
    rows = D // (Q * C)
    cols = weights.shape[1]
    core = lax.axis_index("c")

    grads = replica_grads[0].reshape(Q, C, rows, cols)
    kept = lax.dynamic_index_in_dim(grads, core, 1, False).astype(jnp.float32)
    sent = lax.dynamic_index_in_dim(grads, 1 - core, 1, False).astype(jnp.float32)
    chip = kept + lax.ppermute(sent, "c", SWAP)
    mean_grad = jnp.sum(lax.all_to_all(chip, "q", 0, 0, tiled=True), 0) / (Q * C)

    square = mean_grad * mean_grad + 1e-30
    col_sums = jnp.sum(share(jnp.sum(square, 0)[None], DP, Q * C), (0, 1))
    col_new = decay_rate * col_state + (1.0 - decay_rate) * (col_sums / D)
    col_inv = 1.0 / col_new
    both = jnp.stack([jnp.sum(square, 1), jnp.sum(mean_grad * mean_grad * col_inv, 1)])
    both = jnp.sum(share(both, "z", Z), 0)
    row_new = decay_rate * row_state + (1.0 - decay_rate) * (both[0] / FLAT)
    scaled = mean_grad * lax.rsqrt(row_new[:, None] * col_new[None, :])
    sums = jnp.stack([jnp.sum(row_new), jnp.sum(both[1] / row_new)])
    sums = jnp.pad(sums[None], ((0, 0), (0, 126)))
    totals = jnp.sum(share(sums, DP, Q * C), (0, 1))
    row_mean = totals[0] / D
    rms_value = jnp.sqrt(row_mean * totals[1] / (D * FLAT))
    update = scaled * (jnp.sqrt(row_mean) / jnp.maximum(1.0, rms_value))
    stepped = weights - 0.001 * update
    mine = share(stepped, "q", Q)
    other = lax.ppermute(mine, "c", SWAP)
    first = jnp.where(core == 0, mine, other)
    second = jnp.where(core == 0, other, mine)
    new_weights = jnp.stack([first, second], 1).reshape(D, cols)
    return (new_weights, update, row_new, col_new, rms_value)


def solution(mesh):
    split = Mesh(mesh.devices.reshape(Q, C, Z), ("q", "c", "z"))
    in_specs = (P(DP, None, "z"), P(DP, "z"), P(DP), P("z"))
    out_specs = (P(None, "z"), P(DP, "z"), P(DP), P("z"), P())
    return jax.shard_map(
        per_device, mesh=split, in_specs=in_specs, out_specs=out_specs, check_vma=False
    )
```

time: 386 us -> 115 us (0.30)
  waiting for transfers between devices: 162 us -> 4.52 us
  blocking collectives: 196 us -> 86.4 us
  between operations: 16.6 us -> 3.33 us
  starting transfers between devices: 0.08 us -> 12.7 us
    psum x3 -> x0, blocking collectives: 196 us -> none  [the longest x1 99.5 us: per_device(): clip_total = lax.psum(jnp.sum(raw_update * raw_update), ('dp', 'mp'))]
    reduce_scatter x1 -> x0, waiting for transfers between devices: 109 us -> none  [per_device(): lax.psum_scatter(own_grad, 'dp', scatter_dimension=0, tiled=True)]
    all_to_all x0 -> x5, blocking collectives: none -> 86.4 us  [the longest x4 67 us: share(): lax.all_to_all(jnp.broadcast_to(x[None], (n, *x.shape)), axes, 0, 0, tile...]
    all_gather x1 -> x0, waiting for transfers between devices: 53.7 us -> none  [per_device(): gathered = lax.all_gather(stepped, 'dp', axis=0, tiled=True)]
    ppermute x0 -> x2, starting transfers between devices: none -> 12.7 us  [the longest x1 8.79 us: per_device(): chip = kept + lax.ppermute(sent, 'c', SWAP)]
    ppermute x0 -> x2, waiting for transfers between devices: none -> 4.52 us  [the longest x1 2.26 us: per_device(): chip = kept + lax.ppermute(sent, 'c', SWAP)]
where the time goes in v1:
time: 115 us
  blocking collectives  86.4 us (75%)
  starting transfers between devices  12.7 us (11%)
  other arithmetic  6.93 us (6%)
  waiting for transfers between devices  4.52 us (4%)
  between operations  3.33 us (3%)
    all_to_all x4, blocking collectives, share(): lax.all_to_all(jnp.broadcast_to(x[None], (n, *x.shape)), axes, 0, 0, tile...  67 us
    all_to_all x1, blocking collectives, per_device(): lax.all_to_all(chip, 'q', 0, 0, tiled=True)  19.4 us
    ppermute x1, starting transfers between devices, per_device(): chip = kept + lax.ppermute(sent, 'c', SWAP)  8.79 us
    ppermute x1, starting transfers between devices, per_device(): other = lax.ppermute(mine, 'c', SWAP)  3.9 us
  transfers between devices with their start and end apart: 2, of which 2 were waited for; matrix products, arithmetic and copies ran while one was open for 0% of the time, Pallas kernels for 0%

profile of v1, /device:TPU:1, one launch (start us, length us, event | category | flops | bytes accessed | tf_op | source)
XLA Modules:
  0.0 114.6 jit_solution(16275603829827852554)
XLA Ops:
  0.6 1.1 bitcast_convert_fusion
  1.8 8.8 %collective-permute-start = (f32[16,128,128]{2,1,0:T(8,128)S(1)}, f32[16,128,128]{2,1,0:T(8,128)S(1)}, u32[]{:S(2)}, u32[]{:S(2)}) collective-permute-start(f32[16,128,128]{2,1,0:T(8,128)S(1)} %bitcast_convert_fusion), channel_id=1, source_target_pairs={{0,16},{16,0},{1,17},{17,1},{2,18},{18,2},{3,19},{19,3},{4,20},{20... | collective-permute-start | bytes 3145736 | tf_op jit(solution)/shard_map/ppermute | solution.py:29
  10.6 2.3 %collective-permute-done = f32[16,128,128]{2,1,0:T(8,128)S(1)} collective-permute-done((f32[16,128,128]{2,1,0:T(8,128)S(1)}, f32[16,128,128]{2,1,0:T(8,128)S(1)}, u32[]{:S(2)}, u32[]{:S(2)}) %collective-permute-start) | collective-permute-done | bytes 1048608 | tf_op jit(solution)/shard_map/ppermute | solution.py:29
  12.8 1.2 %convert_add_fusion = f32[16,128,128]{2,1,0:T(8,128)S(1)} fusion(f32[16,128,128]{2,1,0:T(8,128)S(1)} %collective-permute-done, bf16[16,2,128,128]{3,2,1,0:T(8,128)(2,1)} %bitcast.37, s32[]{:T(128)S(6)} %select_n.20), kind=kLoop, calls=%fused_computation.1 | loop fusion | flops 524288 | bytes 2621444 | tf_op jit(solution)/shard_map/add | solution.py:29
  14.0 0.0 copy-start.3
  14.0 0.0 copy-start.4
  14.0 0.0 copy-start
  14.0 19.4 %all_to_all.25 = f32[16,128,128]{2,1,0:T(8,128)S(1)} all-to-all(f32[16,128,128]{2,1,0:T(8,128)S(1)} %convert_add_fusion), channel_id=1, replica_groups=mesh['q'=16,'c'=2,'z'=16] {'q'}, dimensions={0} | all-to-all | bytes 2097152 | tf_op jit(solution)/shard_map/all_to_all | solution.py:30
  33.5 0.1 reduce_sum.81
  33.6 11.3 %all_to_all.26 = f32[32,1,128]{2,1,0:T(1,128)S(1)} all-to-all(f32[32,1,128]{2,1,0:T(1,128)S(1)} %broadcast_in_dim.12), channel_id=1, replica_groups=mesh['q'=16,'c'=2,'z'=16] {'q','c'}, dimensions={0} | all-to-all | bytes 32768 | tf_op jit(solution)/shard_map/all_to_all | solution.py:15
  44.9 0.0 copy-done.3
  44.9 0.0 copy-start.1
  44.9 0.1 add_reduce_fusion.1
  45.0 24.8 %all_to_all.27 = f32[16,2,128]{2,1,0:T(2,128)S(1)} all-to-all(f32[16,2,128]{2,1,0:T(2,128)S(1)} %broadcast_in_dim.13), channel_id=1, replica_groups=mesh['q'=16,'c'=2,'z'=16] {'z'}, dimensions={0} | all-to-all | bytes 32768 | tf_op jit(solution)/shard_map/all_to_all | solution.py:15
  69.8 0.0 copy-done.4
  69.8 0.6 fusion.1
  70.4 0.0 copy-start.2
  70.4 1.4 %maximum_bitcast_fusion = f32[1,2]{1,0:T(1,128)S(1)} fusion(f32[1]{0:T(128)} %bitcast.9, f32[1]{0:T(128)} %bitcast.7), kind=kLoop, calls=%fused_computation.12 | loop fusion | flops 2 | bytes 16 | tf_op jit(solution)/shard_map/broadcast_in_dim | solution.py:41
  71.8 12.1 %all_to_all.28 = f32[32,1,128]{2,1,0:T(1,128)S(1)} all-to-all(f32[32,1,128]{2,1,0:T(1,128)S(1)} %broadcast_in_dim.16), channel_id=1, replica_groups=mesh['q'=16,'c'=2,'z'=16] {'q','c'}, dimensions={0} | all-to-all | bytes 32768 | tf_op jit(solution)/shard_map/all_to_all | solution.py:15
  83.9 0.6 fusion.2
  85.9 0.0 copy-done
  85.9 0.7 multiply_subtract_fusion
  86.7 0.1 broadcast_in_dim.17
  86.8 18.8 %all_to_all.29 = f32[16,128,128]{2,1,0:T(8,128)S(1)} all-to-all(f32[16,128,128]{2,1,0:T(8,128)S(1)} %broadcast_in_dim.17), channel_id=1, replica_groups=mesh['q'=16,'c'=2,'z'=16] {'q'}, dimensions={0} | all-to-all | bytes 2097152 | tf_op jit(solution)/shard_map/all_to_all | solution.py:15
  105.6 3.9 %collective-permute-start.1 = (f32[16,128,128]{2,1,0:T(8,128)S(1)}, f32[16,128,128]{2,1,0:T(8,128)S(1)}, u32[]{:S(2)}, u32[]{:S(2)}) collective-permute-start(f32[16,128,128]{2,1,0:T(8,128)S(1)} %all_to_all.29), channel_id=1, source_target_pairs={{0,16},{16,0},{1,17},{17,1},{2,18},{18,2},{3,19},{19,3},{4,20},{20... | collective-permute-start | bytes 3145736 | tf_op jit(solution)/shard_map/ppermute | solution.py:48
  109.5 2.3 %collective-permute-done.1 = f32[16,128,128]{2,1,0:T(8,128)S(1)} collective-permute-done((f32[16,128,128]{2,1,0:T(8,128)S(1)}, f32[16,128,128]{2,1,0:T(8,128)S(1)}, u32[]{:S(2)}, u32[]{:S(2)}) %collective-permute-start.1) | collective-permute-done | bytes 1048608 | tf_op jit(solution)/shard_map/ppermute | solution.py:48
  111.8 0.2 select_bitcast_fusion.1
  112.0 0.0 copy-done.1
  112.0 0.0 copy-done.2
  112.0 1.5 %pad_maximum_fusion = f32[16,2,128,128]{3,2,1,0:T(8,128)} fusion(f32[16,1,128,128]{3,2,1,0:T(8,128)S(1)} %get-tuple-element.15, f32[16,1,128,128]{3,2,1,0:T(8,128)S(1)} %get-tuple-element.14), kind=kLoop, calls=%fused_computation | loop fusion | flops 524288 | bytes 4194304 | tf_op jit(solution)/shard_map/stack | solution.py:51
  (10 shorter events, 0.2 us)
Async XLA Ops:
  1.8 11.1 %collective-permute-start = (f32[16,128,128]{2,1,0:T(8,128)S(1)}, f32[16,128,128]{2,1,0:T(8,128)S(1)}, u32[]{:S(2)}, u32[]{:S(2)}) collective-permute-start(f32[16,128,128]{2,1,0:T(8,128)S(1)} %bitcast_convert_fusion), channel_id=1, source_target_pairs={{0,16},{16,0},{1,17},{17,1},{2,18},{18,2},{3,19},{19,3},{4,20},{20... | collective-permute-start | bytes 3145736 | tf_op jit(solution)/shard_map/ppermute | solution.py:29
  14.0 30.9 %copy-start.3 = (f32[128]{0:T(128)S(1)}, f32[128]{0:T(128)}, u32[]{:S(2)}) copy-start(f32[128]{0:T(128)} %param.7) | copy-start | bytes 1540
  14.0 55.8 %copy-start.4 = (f32[128]{0:T(128)S(1)}, f32[128]{0:T(128)}, u32[]{:S(2)}) copy-start(f32[128]{0:T(128)} %param.6) | copy-start | bytes 1540
  14.0 71.9 %copy-start = (f32[128,128]{1,0:T(8,128)S(1)}, f32[128,128]{1,0:T(8,128)}, u32[]{:S(2)}) copy-start(f32[128,128]{1,0:T(8,128)} %param.5) | copy-start | bytes 196612
  44.9 67.1 %copy-start.1 = (f32[128]{0:T(128)}, f32[128]{0:T(128)S(1)}, u32[]{:S(2)}) copy-start(f32[128]{0:T(128)S(1)} %get-tuple-element.13) | copy-start | bytes 1540
  70.4 41.5 %copy-start.2 = (f32[128]{0:T(128)}, f32[128]{0:T(128)S(1)}, u32[]{:S(2)}) copy-start(f32[128]{0:T(128)S(1)} %get-tuple-element.11) | copy-start | bytes 1540
  105.6 6.2 %collective-permute-start.1 = (f32[16,128,128]{2,1,0:T(8,128)S(1)}, f32[16,128,128]{2,1,0:T(8,128)S(1)}, u32[]{:S(2)}, u32[]{:S(2)}) collective-permute-start(f32[16,128,128]{2,1,0:T(8,128)S(1)} %all_to_all.29), channel_id=1, source_target_pairs={{0,16},{16,0},{1,17},{17,1},{2,18},{18,2},{3,19},{19,3},{4,20},{20... | collective-permute-start | bytes 3145736 | tf_op jit(solution)/shard_map/ppermute | solution.py:48

commit v2 on v1

v2 whole, which is shorter than its diff:
```python
import jax
import jax.numpy as jnp
from jax import lax
from jax.experimental import pallas as pl
from jax.experimental.pallas import tpu as pltpu
from jax.sharding import Mesh, PartitionSpec as P

D = 4096
STEP = 10
FLAT = 2048
Q, C, Z = 16, 2, 16
ROWS = D // (Q * C)
COLS = FLAT // Z
CHUNKS = 4
DP = ("q", "c")
SWAP = [(0, 1), (1, 0)]
VMEM = pl.BlockSpec(memory_space=pltpu.VMEM)
HBM = pl.BlockSpec(memory_space=pltpu.HBM)
ANY = pl.BlockSpec(memory_space=pl.ANY)


def share(x, axes, n):
    return lax.all_to_all(
        jnp.broadcast_to(x[None], (n, *x.shape)), axes, 0, 0, tiled=True
    )


def sent_body(grads, sent, held, sems):
    core = lax.axis_index("c")
    part = Q // CHUNKS
    copies = []
    for i in range(CHUNKS):
        at = pl.ds(i * part, part)
        copies.append(
            pltpu.make_async_copy(grads.at[at, 1 - core], held.at[at], sems.at[i])
        )
        copies[i].start()
    for i in range(CHUNKS):
        at = pl.ds(i * part, part)
        copies[i].wait()
        sent[at] = held[at].astype(jnp.float32)


def sent_rows(grads):
    shape = (Q, ROWS, COLS)
    return pl.pallas_call(
        sent_body,
        out_shape=jax.ShapeDtypeStruct(shape, jnp.float32),
        in_specs=[HBM],
        out_specs=VMEM,
        scratch_shapes=[
            pltpu.VMEM(shape, grads.dtype),
            pltpu.SemaphoreType.DMA((CHUNKS,)),
        ],
        compiler_params=pltpu.CompilerParams(vmem_limit_bytes=16 * 2**20),
        name="sent_rows",
    )(grads)


def step_body(parts, scaled, weights, update, stepped, rms):
    totals = jnp.sum(jnp.sum(parts[...], 0), 1, keepdims=True)
    row_mean = totals[0:1] / D
    rms_value = jnp.sqrt(row_mean * totals[1:2] / (D * FLAT))
    gain = jnp.sqrt(row_mean) / jnp.maximum(1.0, rms_value)
    new = scaled[...] * gain
    update[...] = new
    after = weights[...] - 0.001 * new
    for i in range(Q):
        stepped[i] = after
    rms[...] = rms_value


def step(parts, scaled, weights):
    return pl.pallas_call(
        step_body,
        out_shape=(
            jax.ShapeDtypeStruct((ROWS, COLS), jnp.float32),
            jax.ShapeDtypeStruct((Q, ROWS, COLS), jnp.float32),
            jax.ShapeDtypeStruct((1, 1), jnp.float32),
        ),
        in_specs=[VMEM, VMEM, VMEM],
        out_specs=(VMEM, VMEM, VMEM),
        compiler_params=pltpu.CompilerParams(vmem_limit_bytes=16 * 2**20),
        name="step",
    )(parts, scaled, weights)


def lay_mine_body(mine, whole, sem):
    copy = pltpu.make_async_copy(mine, whole.at[:, lax.axis_index("c")], sem)
    copy.start()
    copy.wait()


def lay_other_body(other, half, whole, sem):
    copy = pltpu.make_async_copy(other, whole.at[:, 1 - lax.axis_index("c")], sem)
    copy.start()
    copy.wait()


def lay(body, *operands):
    return pl.pallas_call(
        body,
        out_shape=jax.ShapeDtypeStruct((Q, C, ROWS, COLS), jnp.float32),
        in_specs=[ANY, HBM][: len(operands)],
        out_specs=HBM,
        input_output_aliases={1: 0} if len(operands) == 2 else {},
        scratch_shapes=[pltpu.SemaphoreType.DMA],
        compiler_params=pltpu.CompilerParams(vmem_limit_bytes=16 * 2**20),
        cost_estimate=pl.CostEstimate(
            flops=0, bytes_accessed=2 * Q * ROWS * COLS * 4, transcendentals=0
        ),
        name="lay",
    )(*operands)


def per_device(replica_grads, weights, row_state, col_state):
    decay_rate = 1.0 - float(STEP) ** (-0.8)

    grads = replica_grads.reshape(Q, C, ROWS, COLS)
    other = lax.ppermute(sent_rows(grads), "c", SWAP)
    kept = lax.dynamic_index_in_dim(grads, lax.axis_index("c"), 1, False)
    kept = lax.optimization_barrier(kept.astype(jnp.float32))
    chip = kept + other
    mean_grad = jnp.sum(lax.all_to_all(chip, "q", 0, 0, tiled=True), 0) / (Q * C)

    square = mean_grad * mean_grad + 1e-30
    col_sums = jnp.sum(share(jnp.sum(square, 0)[None], DP, Q * C), (0, 1))
    col_new = decay_rate * col_state + (1.0 - decay_rate) * (col_sums / D)
    both = jnp.stack(
        [jnp.sum(square, 1), jnp.sum(mean_grad * mean_grad * (1.0 / col_new), 1)]
    )
    both = jnp.sum(share(both, "z", Z), 0)
    row_new = decay_rate * row_state + (1.0 - decay_rate) * (both[0] / FLAT)
    scaled = mean_grad * lax.rsqrt(row_new[:, None] * col_new[None, :])
    parts = jnp.stack([row_new, both[1] / row_new])
    parts, scaled = lax.optimization_barrier((parts, scaled))
    parts = share(parts, DP, Q * C)
    update, stepped, rms_value = step(parts, scaled, weights)
    mine = lax.all_to_all(stepped, "q", 0, 0, tiled=True)
    other = lax.ppermute(mine, "c", SWAP)
    half = lay(lay_mine_body, mine)
    new_weights = lay(lay_other_body, other, half).reshape(D, COLS)
    return (new_weights, update, row_new, col_new, rms_value.reshape(()))


def solution(mesh):
    split_mesh = Mesh(mesh.devices.reshape(Q, C, Z), ("q", "c", "z"))
    in_specs = (P(DP, None, "z"), P(DP, "z"), P(DP), P("z"))
    out_specs = (P(None, "z"), P(DP, "z"), P(DP), P("z"), P())
    return jax.shard_map(
        per_device,
        mesh=split_mesh,
        in_specs=in_specs,
        out_specs=out_specs,
        check_vma=False,
    )
```

time: 115 us -> 109 us (0.948)
  other arithmetic: 6.93 us -> 0.6 us
  Pallas kernels: 0 us -> 3.05 us
  between operations: 3.33 us -> 0.82 us
    all_to_all x0 -> x1, blocking collectives: none -> 19 us  [per_device(): mine = lax.all_to_all(stepped, 'q', 0, 0, tiled=True)]
    all_to_all x4 -> x3, blocking collectives: 67 us -> 48.4 us  [share(): lax.all_to_all(jnp.broadcast_to(x[None], (n, *x.shape)), axes, 0, 0, tile...]
    pallas_call x0 -> x4, Pallas kernels: none -> 3.05 us  [the longest x2 1.97 us: lay(): pl.pallas_call(body, out_shape=jax.ShapeDtypeStruct((Q, C, ROWS, COLS), j...]
    another operation x3, other arithmetic: 1.66 us -> 0.03 us  [the longest x2 0.02 us: per_device(): parts = jnp.stack([row_new, both[1] / row_new])]
    broadcast_in_dim x1 -> x0, other arithmetic: 1.37 us -> none  [per_device(): sums = jnp.pad(sums[None], ((0, 0), (0, 126)))]
    unnamed x10 -> x14, local copies, waits for them, and re-layouts: 0.03 us -> 1.25 us
  transfers between devices with their start and end apart: 2 -> 2, of which waited for: 2 -> 2; matrix products, arithmetic and copies ran while one was open for 0% -> 0% of each run, Pallas kernels for 0% -> 1%
where the time goes in v2:
time: 109 us
  blocking collectives  86.8 us (80%)
  starting transfers between devices  12.7 us (12%)
  waiting for transfers between devices  3.39 us (3%)
  Pallas kernels  3.05 us (3%)
  local copies, waits for them, and re-layouts  1.28 us (1%)
    all_to_all x3, blocking collectives, share(): lax.all_to_all(jnp.broadcast_to(x[None], (n, *x.shape)), axes, 0, 0, tile...  48.4 us
    all_to_all x1, blocking collectives, per_device(): lax.all_to_all(chip, 'q', 0, 0, tiled=True)  19.4 us
    all_to_all x1, blocking collectives, per_device(): mine = lax.all_to_all(stepped, 'q', 0, 0, tiled=True)  19 us
    ppermute x1, starting transfers between devices, per_device(): other = lax.ppermute(sent_rows(grads), 'c', SWAP)  8.92 us
    ppermute x1, starting transfers between devices, per_device(): other = lax.ppermute(mine, 'c', SWAP)  3.75 us
  transfers between devices with their start and end apart: 2, of which 2 were waited for; matrix products, arithmetic and copies ran while one was open for 0% of the time, Pallas kernels for 1%

profile of v2, /device:TPU:1, one launch (start us, length us, event | category | flops | bytes accessed | tf_op | source)
XLA Modules:
  0.0 108.6 jit_solution(2258107052804295939)
XLA Ops:
  0.6 0.0 copy-start
  0.6 1.2 %copy-done = bf16[1,4096,128]{2,1,0:T(8,128)(2,1)S(1)} copy-done((bf16[1,4096,128]{2,1,0:T(8,128)(2,1)S(1)}, bf16[1,4096,128]{2,1,0:T(8,128)(2,1)}, u32[]{:S(2)}) %copy-start) | copy-done | bytes 1048600
  1.9 0.0 copy-start.1
  1.9 0.3 sent_rows.1
  2.1 8.9 %collective-permute-start = (f32[16,128,128]{2,1,0:T(8,128)S(1)}, f32[16,128,128]{2,1,0:T(8,128)S(1)}, u32[]{:S(2)}, u32[]{:S(2)}) collective-permute-start(f32[16,128,128]{2,1,0:T(8,128)S(1)} %sent_rows.1), channel_id=1, source_target_pairs={{0,16},{16,0},{1,17},{17,1},{2,18},{18,2},{3,19},{19,3},{4,20},{20... | collective-permute-start | bytes 3145736 | tf_op jit(solution)/shard_map/ppermute | solution.py:120
  11.1 0.0 copy-done.1
  11.1 0.1 bitcast_convert_fusion
  11.2 2.1 %collective-permute-done = f32[16,128,128]{2,1,0:T(8,128)S(1)} collective-permute-done((f32[16,128,128]{2,1,0:T(8,128)S(1)}, f32[16,128,128]{2,1,0:T(8,128)S(1)}, u32[]{:S(2)}, u32[]{:S(2)}) %collective-permute-start) | collective-permute-done | bytes 1048608 | tf_op jit(solution)/shard_map/ppermute | solution.py:120
  13.3 0.1 add.20
  13.5 0.0 copy-start.6
  13.5 0.0 copy-start.5
  13.5 0.0 copy-start.2
  13.5 19.4 %all_to_all.25 = f32[16,128,128]{2,1,0:T(8,128)S(1)} all-to-all(f32[16,128,128]{2,1,0:T(8,128)S(1)} %add.20), channel_id=1, replica_groups=mesh['q'=16,'c'=2,'z'=16] {'q'}, dimensions={0} | all-to-all | bytes 2097152 | tf_op jit(solution)/shard_map/all_to_all | solution.py:124
  32.9 0.1 reduce_sum.54
  33.0 11.3 %all_to_all.26 = f32[32,1,128]{2,1,0:T(1,128)S(1)} all-to-all(f32[32,1,128]{2,1,0:T(1,128)S(1)} %broadcast_in_dim.6), channel_id=1, replica_groups=mesh['q'=16,'c'=2,'z'=16] {'q','c'}, dimensions={0} | all-to-all | bytes 32768 | tf_op jit(solution)/shard_map/all_to_all | solution.py:23
  44.3 0.0 copy-done.6
  44.3 0.0 copy-start.4
  44.4 0.1 add_reduce_fusion.1
  44.5 24.8 %all_to_all.27 = f32[16,2,128]{2,1,0:T(2,128)S(1)} all-to-all(f32[16,2,128]{2,1,0:T(2,128)S(1)} %broadcast_in_dim.7), channel_id=1, replica_groups=mesh['q'=16,'c'=2,'z'=16] {'z'}, dimensions={0} | all-to-all | bytes 32768 | tf_op jit(solution)/shard_map/all_to_all | solution.py:23
  69.3 0.0 copy-done.5
  69.3 0.0 copy-start.3
  69.3 0.1 rsqrt_multiply_fusion.scaled
  69.4 12.4 %all_to_all.28.parts = f32[32,2,128]{2,1,0:T(2,128)S(1)} all-to-all(f32[32,2,128]{2,1,0:T(2,128)S(1)} %broadcast_in_dim.8), channel_id=1, replica_groups=mesh['q'=16,'c'=2,'z'=16] {'q','c'}, dimensions={0} | all-to-all | bytes 65536 | tf_op jit(solution)/shard_map/all_to_all | solution.py:23
  81.8 0.0 copy-done.2
  81.8 0.8 step.1
  82.6 19.0 %all_to_all.29.mine = f32[16,128,128]{2,1,0:T(8,128)S(1)} all-to-all(f32[16,128,128]{2,1,0:T(8,128)S(1)} %get-tuple-element.12), channel_id=1, replica_groups=mesh['q'=16,'c'=2,'z'=16] {'q'}, dimensions={0} | all-to-all | bytes 2097152 | tf_op jit(solution)/shard_map/all_to_all | solution.py:139
  101.6 3.7 %collective-permute-start.1 = (f32[16,128,128]{2,1,0:T(8,128)S(1)}, f32[16,128,128]{2,1,0:T(8,128)S(1)}, u32[]{:S(2)}, u32[]{:S(2)}) collective-permute-start(f32[16,128,128]{2,1,0:T(8,128)S(1)} %all_to_all.29.mine), channel_id=1, source_target_pairs={{0,16},{16,0},{1,17},{17,1},{2,18},{18,2},{3,19},{19,3},{4,20},{20... | collective-permute-start | bytes 3145736 | tf_op jit(solution)/shard_map/ppermute | solution.py:140
  105.4 1.0 lay.2.half
  106.4 0.0 copy-done.4
  106.4 0.0 copy-done.3
  106.4 1.2 %collective-permute-done.1.other = f32[16,128,128]{2,1,0:T(8,128)S(1)} collective-permute-done((f32[16,128,128]{2,1,0:T(8,128)S(1)}, f32[16,128,128]{2,1,0:T(8,128)S(1)}, u32[]{:S(2)}, u32[]{:S(2)}) %collective-permute-start.1) | collective-permute-done | bytes 1048608 | tf_op jit(solution)/shard_map/ppermute | solution.py:140
  107.6 1.0 lay.3
  (10 shorter events, 0.1 us)
Async XLA Ops:
  0.6 1.2 %copy-start = (bf16[1,4096,128]{2,1,0:T(8,128)(2,1)S(1)}, bf16[1,4096,128]{2,1,0:T(8,128)(2,1)}, u32[]{:S(2)}) copy-start(bf16[1,4096,128]{2,1,0:T(8,128)(2,1)} %param.4) | copy-start | bytes 3145732
  1.9 9.2 %copy-start.1 = (bf16[1,4096,128]{2,1,0:T(8,128)(2,1)S(1)}, bf16[1,4096,128]{2,1,0:T(8,128)(2,1)}, u32[]{:S(2)}) copy-start(bf16[1,4096,128]{2,1,0:T(8,128)(2,1)} %param.4) | copy-start | bytes 3145732
  2.1 11.2 %collective-permute-start = (f32[16,128,128]{2,1,0:T(8,128)S(1)}, f32[16,128,128]{2,1,0:T(8,128)S(1)}, u32[]{:S(2)}, u32[]{:S(2)}) collective-permute-start(f32[16,128,128]{2,1,0:T(8,128)S(1)} %sent_rows.1), channel_id=1, source_target_pairs={{0,16},{16,0},{1,17},{17,1},{2,18},{18,2},{3,19},{19,3},{4,20},{20... | collective-permute-start | bytes 3145736 | tf_op jit(solution)/shard_map/ppermute | solution.py:120
  13.5 30.9 %copy-start.6 = (f32[128]{0:T(128)S(1)}, f32[128]{0:T(128)}, u32[]{:S(2)}) copy-start(f32[128]{0:T(128)} %param.7) | copy-start | bytes 1540
  13.5 55.8 %copy-start.5 = (f32[128]{0:T(128)S(1)}, f32[128]{0:T(128)}, u32[]{:S(2)}) copy-start(f32[128]{0:T(128)} %param.6) | copy-start | bytes 1540
  13.5 68.3 %copy-start.2 = (f32[128,128]{1,0:T(8,128)S(1)}, f32[128,128]{1,0:T(8,128)}, u32[]{:S(2)}) copy-start(f32[128,128]{1,0:T(8,128)} %weights.1) | copy-start | bytes 196612
  44.3 62.0 %copy-start.4 = (f32[128]{0:T(128)}, f32[128]{0:T(128)S(1)}, u32[]{:S(2)}) copy-start(f32[128]{0:T(128)S(1)} %get-tuple-element.20) | copy-start | bytes 1540
  69.3 37.1 %copy-start.3 = (f32[128]{0:T(128)}, f32[128]{0:T(128)S(1)}, u32[]{:S(2)}) copy-start(f32[128]{0:T(128)S(1)} %get-tuple-element.18) | copy-start | bytes 1540
  101.6 6.0 %collective-permute-start.1 = (f32[16,128,128]{2,1,0:T(8,128)S(1)}, f32[16,128,128]{2,1,0:T(8,128)S(1)}, u32[]{:S(2)}, u32[]{:S(2)}) collective-permute-start(f32[16,128,128]{2,1,0:T(8,128)S(1)} %all_to_all.29.mine), channel_id=1, source_target_pairs={{0,16},{16,0},{1,17},{17,1},{2,18},{18,2},{3,19},{19,3},{4,20},{20... | collective-permute-start | bytes 3145736 | tf_op jit(solution)/shard_map/ppermute | solution.py:140

commit v3 on v2

--- a/solution.py
+++ b/solution.py
@@ -1,3 +1,5 @@
+import functools
+
 import jax
 import jax.numpy as jnp
 from jax import lax
@@ -12,6 +14,7 @@
 ROWS = D // (Q * C)
 COLS = FLAT // Z
 CHUNKS = 4
+AHEAD = (128, 96, 64, 0)
 DP = ("q", "c")
 SWAP = [(0, 1), (1, 0)]
 VMEM = pl.BlockSpec(memory_space=pltpu.VMEM)
@@ -85,32 +88,121 @@
     )(parts, scaled, weights)
 
 
-def lay_mine_body(mine, whole, sem):
-    copy = pltpu.make_async_copy(mine, whole.at[:, lax.axis_index("c")], sem)
-    copy.start()
-    copy.wait()
-
-
-def lay_other_body(other, half, whole, sem):
-    copy = pltpu.make_async_copy(other, whole.at[:, 1 - lax.axis_index("c")], sem)
-    copy.start()
-    copy.wait()
-
-
-def lay(body, *operands):
-    return pl.pallas_call(
-        body,
-        out_shape=jax.ShapeDtypeStruct((Q, C, ROWS, COLS), jnp.float32),
-        in_specs=[ANY, HBM][: len(operands)],
-        out_specs=HBM,
-        input_output_aliases={1: 0} if len(operands) == 2 else {},
-        scratch_shapes=[pltpu.SemaphoreType.DMA],
-        compiler_params=pltpu.CompilerParams(vmem_limit_bytes=16 * 2**20),
-        cost_estimate=pl.CostEstimate(
-            flops=0, bytes_accessed=2 * Q * ROWS * COLS * 4, transcendentals=0
+def lay_body(mine, other, new, rms, row, whole, update, rms_out, row_out, sems):
+    core = lax.axis_index("c")
+    copies = [
+        pltpu.make_async_copy(mine, whole.at[:, core], sems.at[0]),
+        pltpu.make_async_copy(other, whole.at[:, 1 - core], sems.at[1]),
+        pltpu.make_async_copy(new, update, sems.at[2]),
+        pltpu.make_async_copy(rms, rms_out, sems.at[3]),
+        pltpu.make_async_copy(row, row_out, sems.at[4]),
+    ]
+    for copy in copies:
+        copy.start()
+    for copy in copies:
+        copy.wait()
+
+
+def lay(mine, other, new, rms, row):
+    return pl.pallas_call(
+        lay_body,
+        out_shape=(
+            jax.ShapeDtypeStruct((Q, C, ROWS, COLS), jnp.float32),
+            jax.ShapeDtypeStruct((ROWS, COLS), jnp.float32),
+            jax.ShapeDtypeStruct((1, 1), jnp.float32),
+            jax.ShapeDtypeStruct((1, ROWS), jnp.float32),
         ),
+        in_specs=[ANY] * 5,
+        out_specs=(HBM,) * 4,
+        scratch_shapes=[pltpu.SemaphoreType.DMA((5,))],
+        compiler_params=pltpu.CompilerParams(vmem_limit_bytes=16 * 2**20),
         name="lay",
-    )(*operands)
+    )(mine, other, new, rms, row)
+
+
+def finish_body(ahead, mine, other, own, others, scaled, row, whole, update, rms, row_out, out, sems):
+    core = lax.axis_index("c")
+    part = Q // CHUNKS
+    tail = pl.ds(ROWS, 8)
+    parts = jnp.sum(mine[:, tail], 0) + jnp.sum(other[:, tail], 0)
+    totals = jnp.sum(parts[0:2], 1, keepdims=True)
+    row_mean = totals[0:1] / D
+    rms_value = jnp.sqrt(row_mean * totals[1:2] / (D * FLAT))
+    gain = jnp.sqrt(row_mean) / jnp.maximum(1.0, rms_value)
+    rms[...] = rms_value
+    row_out[...] = row[...]
+    lowered = 0.001 * gain
+    writes = []
+    for i in range(CHUNKS):
+        for j in range(i * part, (i + 1) * part):
+            for side, rows, known in ((core, mine, own), (1 - core, other, others)):
+                out[j, side, :ahead] = known[j] - lowered * rows[j, :ahead]
+                if ahead < ROWS:
+                    out[j, side, ahead:] = (
+                        rows[j, ROWS + 8 :] - lowered * rows[j, ahead:ROWS]
+                    )
+        at = pl.ds(i * part, part)
+        writes.append(pltpu.make_async_copy(out.at[at], whole.at[at], sems.at[i]))
+        writes[i].start()
+    update[...] = scaled[...] * gain
+    for i in range(CHUNKS):
+        writes[i].wait()
+
+
+def finish(ahead, mine, other, own, others, scaled, row):
+    whole = (Q, C, ROWS, COLS)
+    return pl.pallas_call(
+        functools.partial(finish_body, ahead),
+        out_shape=(
+            jax.ShapeDtypeStruct(whole, jnp.float32),
+            jax.ShapeDtypeStruct((ROWS, COLS), jnp.float32),
+            jax.ShapeDtypeStruct((1, 1), jnp.float32),
+            jax.ShapeDtypeStruct((1, ROWS), jnp.float32),
+        ),
+        in_specs=[VMEM] * 6,
+        out_specs=(HBM, VMEM, VMEM, VMEM),
+        scratch_shapes=[
+            pltpu.VMEM(whole, jnp.float32),
+            pltpu.SemaphoreType.DMA((CHUNKS,)),
+        ],
+        compiler_params=pltpu.CompilerParams(vmem_limit_bytes=16 * 2**20),
+        name="finish",
+    )(mine, other, own, others, scaled, row)
+
+
+def front(ahead, chip, weights):
+    sent = chip
+    if ahead:
+        rows = jnp.broadcast_to(weights[None, :ahead], (Q, ahead, COLS))
+        sent = jnp.concatenate([chip, rows], 1)
+    got = lax.all_to_all(sent, "q", 0, 0, tiled=True)
+    rows = jnp.pad(got[:, ROWS:], ((0, 0), (0, ROWS - ahead), (0, 0)))
+    return jnp.sum(got[:, :ROWS], 0) / (Q * C), rows
+
+
+def back(ahead, scaled, parts, row, weights, own_weights):
+    if ahead:
+        outs = back_early(ahead, scaled, parts, row, weights, own_weights)
+    else:
+        outs = back_late(scaled, parts, row, weights)
+    return outs[0].reshape(D, COLS), outs[1], outs[2].reshape(()), outs[3][0]
+
+
+def back_early(ahead, scaled, parts, row, weights, own_weights):
+    own = own_weights[:, :ahead]
+    others = lax.ppermute(own, "c", SWAP)
+    empty = jnp.zeros((6, COLS), jnp.float32)
+    mine = share(jnp.concatenate([scaled, parts, empty, weights[ahead:]]), "q", Q)
+    other = lax.ppermute(mine, "c", SWAP)
+    return finish(ahead, mine, other, own, others, scaled, row)
+
+
+def back_late(scaled, parts, row, weights):
+    parts = share(parts, DP, Q * C)
+    new, stepped, rms = step(parts, scaled, weights)
+    mine = lax.all_to_all(stepped, "q", 0, 0, tiled=True)
+    other = lax.ppermute(mine, "c", SWAP)
+    return lay(mine, other, new, rms, row)
 
 
 def per_device(replica_grads, weights, row_state, col_state):
@@ -121,7 +213,10 @@
     kept = lax.dynamic_index_in_dim(grads, lax.axis_index("c"), 1, False)
     kept = lax.optimization_barrier(kept.astype(jnp.float32))
     chip = kept + other
-    mean_grad = jnp.sum(lax.all_to_all(chip, "q", 0, 0, tiled=True), 0) / (Q * C)
+    plane = jnp.minimum(lax.axis_index("z") // 2, len(AHEAD) - 1)
+    mean_grad, own_weights = lax.switch(
+        plane, [functools.partial(front, n) for n in AHEAD], chip, weights
+    )
 
     square = mean_grad * mean_grad + 1e-30
     col_sums = jnp.sum(share(jnp.sum(square, 0)[None], DP, Q * C), (0, 1))
@@ -133,14 +228,12 @@
     row_new = decay_rate * row_state + (1.0 - decay_rate) * (both[0] / FLAT)
     scaled = mean_grad * lax.rsqrt(row_new[:, None] * col_new[None, :])
     parts = jnp.stack([row_new, both[1] / row_new])
-    parts, scaled = lax.optimization_barrier((parts, scaled))
-    parts = share(parts, DP, Q * C)
-    update, stepped, rms_value = step(parts, scaled, weights)
-    mine = lax.all_to_all(stepped, "q", 0, 0, tiled=True)
-    other = lax.ppermute(mine, "c", SWAP)
-    half = lay(lay_mine_body, mine)
-    new_weights = lay(lay_other_body, other, half).reshape(D, COLS)
-    return (new_weights, update, row_new, col_new, rms_value.reshape(()))
+    new_weights, update, rms_value, row_new = lax.switch(
+        plane,
+        [functools.partial(back, n) for n in AHEAD],
+        *(scaled, parts, row_new[None], weights, own_weights),
+    )
+    return (new_weights, update, row_new, col_new, rms_value)
 
 
 def solution(mesh):

time: 109 us -> 101 us (0.927)
  blocking collectives: 86.8 us -> 74.4 us
  starting transfers between devices: 12.7 us -> 16 us
  waiting for transfers between devices: 3.39 us -> 4.74 us
    all_to_all x2 -> x1, blocking collectives: 38.4 us -> 30.6 us  [front(): got = lax.all_to_all(sent, 'q', 0, 0, tiled=True)]
    all_to_all x3, blocking collectives: 48.4 us -> 43.8 us  [share(): lax.all_to_all(jnp.broadcast_to(x[None], (n, *x.shape)), axes, 0, 0, tile...]
    ppermute x1 -> x2, starting transfers between devices: 3.75 us -> 7.09 us  [the longest x1 5.17 us: back_early(): other = lax.ppermute(mine, 'c', SWAP)]
    ppermute x1 -> x2, waiting for transfers between devices: 1.25 us -> 2.63 us  [the longest x1 2.63 us: back_early(): others = lax.ppermute(own, 'c', SWAP)]
    pallas_call x3 -> x1, Pallas kernels: 2.78 us -> 2.18 us  [finish(): pl.pallas_call(functools.partial(finish_body, ahead), out_shape=(jax.Shap...]
  transfers between devices with their start and end apart: 2 -> 3, of which waited for: 2 -> 2; matrix products, arithmetic and copies ran while one was open for 0% -> 0% of each run, Pallas kernels for 1% -> 0%
where the time goes in v3:
time: 101 us
  blocking collectives  74.4 us (74%)
  starting transfers between devices  16 us (16%)
  waiting for transfers between devices  4.74 us (5%)
  Pallas kernels  2.45 us (2%)
  local copies, waits for them, and re-layouts  1.51 us (1%)
    all_to_all x3, blocking collectives, share(): lax.all_to_all(jnp.broadcast_to(x[None], (n, *x.shape)), axes, 0, 0, tile...  43.8 us
    all_to_all x1, blocking collectives, front(): got = lax.all_to_all(sent, 'q', 0, 0, tiled=True)  30.6 us
    ppermute x1, starting transfers between devices, per_device(): other = lax.ppermute(sent_rows(grads), 'c', SWAP)  8.92 us
    ppermute x1, starting transfers between devices, back_early(): other = lax.ppermute(mine, 'c', SWAP)  5.17 us
    ppermute x1, waiting for transfers between devices, back_early(): others = lax.ppermute(own, 'c', SWAP)  2.63 us
    pallas_call x1, Pallas kernels, finish(): pl.pallas_call(functools.partial(finish_body, ahead), out_shape=(jax.Shap...  2.18 us
    ppermute x1, waiting for transfers between devices, per_device(): other = lax.ppermute(sent_rows(grads), 'c', SWAP)  2.11 us
  transfers between devices with their start and end apart: 3, of which 2 were waited for; matrix products, arithmetic and copies ran while one was open for 0% of the time, Pallas kernels for 0%

profile of v3, /device:TPU:1, one launch (start us, length us, event | category | flops | bytes accessed | tf_op | source)
XLA Modules:
  0.0 101.1 jit_solution(2510536899357824015)
XLA Ops:
  0.6 0.0 copy-start
  0.6 1.2 %copy-done = bf16[1,4096,128]{2,1,0:T(8,128)(2,1)S(1)} copy-done((bf16[1,4096,128]{2,1,0:T(8,128)(2,1)S(1)}, bf16[1,4096,128]{2,1,0:T(8,128)(2,1)}, u32[]{:S(2)}) %copy-start) | copy-done | bytes 1048600
  1.9 0.0 copy-start.1
  1.9 0.3 sent_rows.1
  2.1 8.9 %collective-permute-start.7 = (f32[16,128,128]{2,1,0:T(8,128)S(1)}, f32[16,128,128]{2,1,0:T(8,128)S(1)}, u32[]{:S(2)}, u32[]{:S(2)}) collective-permute-start(f32[16,128,128]{2,1,0:T(8,128)S(1)} %sent_rows.1), channel_id=1, source_target_pairs={{0,16},{16,0},{1,17},{17,1},{2,18},{18,2},{3,19},{19,3},{4,20},{20... | collective-permute-start | bytes 3145736 | tf_op jit(solution)/shard_map/ppermute | solution.py:212
  11.1 0.0 copy-done.1
  11.1 0.1 bitcast_convert_fusion
  11.2 0.0 copy-start.2
  11.2 2.1 %collective-permute-done.7 = f32[16,128,128]{2,1,0:T(8,128)S(1)} collective-permute-done((f32[16,128,128]{2,1,0:T(8,128)S(1)}, f32[16,128,128]{2,1,0:T(8,128)S(1)}, u32[]{:S(2)}, u32[]{:S(2)}) %collective-permute-start.7) | collective-permute-done | bytes 1048608 | tf_op jit(solution)/shard_map/ppermute | solution.py:212
  13.3 0.1 add.28
  13.5 0.0 copy-done.2
  13.5 0.0 copy-start.5
  13.5 0.0 copy-start.4
  13.5 31.1 %conditional.2 = (f32[128,128]{1,0:T(8,128)S(1)}, f32[16,128,128]{2,1,0:T(8,128)S(1)}, f32[128,128]{1,0:T(8,128)S(1)}) conditional(s32[]{:T(128)} %clamp.4, (f32[128,128]{1,0:T(8,128)S(1)}, f32[16,128,128]{2,1,0:T(8,128)S(1)}) %tuple.87, (f32[128,128]{1,0:T(8,128)S(1)}, f32[16,128,128]{2,1,0:T(8,128)S(1)}) %tuple.88, ...), branch_computations={%region_0.2_spmd, %region_2.4_spmd, %region_4.6_spmd, %region_6.8_... | conditional | flops 802816 | bytes 12992540 | solution.py:217
  13.5 0.1 broadcast_in_dim.10
  13.6 0.2 pad_maximum_fusion
  13.8 30.6 %all_to_all.46 = f32[16,256,128]{2,1,0:T(8,128)S(1)} all-to-all(f32[16,256,128]{2,1,0:T(8,128)S(1)} %pad_maximum_fusion), channel_id=1, replica_groups=mesh['q'=16,'c'=2,'z'=16] {'q'}, dimensions={0} | all-to-all | bytes 4194304 | tf_op jit(solution)/shard_map/cond/branch_0_fun/all_to_all | solution.py:178
  44.4 0.1 fusion.5
  44.6 0.1 add_reduce_fusion.1
  44.7 11.3 %all_to_all.55 = f32[32,1,128]{2,1,0:T(1,128)S(1)} all-to-all(f32[32,1,128]{2,1,0:T(1,128)S(1)} %broadcast_in_dim.30), channel_id=1, replica_groups=mesh['q'=16,'c'=2,'z'=16] {'q','c'}, dimensions={0} | all-to-all | bytes 32768 | tf_op jit(solution)/shard_map/all_to_all | solution.py:26
  56.0 0.0 copy-done.5
  56.0 0.0 copy-start.3
  56.0 0.1 multiply_reduce_fusion
  56.1 13.8 %all_to_all.56 = f32[16,2,128]{2,1,0:T(2,128)S(1)} all-to-all(f32[16,2,128]{2,1,0:T(2,128)S(1)} %broadcast_in_dim.31), channel_id=1, replica_groups=mesh['q'=16,'c'=2,'z'=16] {'z'}, dimensions={0} | all-to-all | bytes 32768 | tf_op jit(solution)/shard_map/all_to_all | solution.py:26
  70.0 0.0 copy-done.4
  70.0 0.1 rsqrt_multiply_fusion
  70.1 0.0 copy-done.3
  70.1 31.0 %conditional.3 = ((f32[16,2,128,128]{3,2,1,0:T(8,128)}, f32[128,128]{1,0:T(8,128)}, f32[1,1]{1,0:T(1,128)}, f32[1,128]{1,0:T(1,128)})) conditional(s32[]{:T(128)} %clamp.4, (f32[128,128]{1,0:T(8,128)S(1)}, f32[2,128]{1,0:T(2,128)S(1)}, f32[16,128,128]{2,1,0:T(8,128)S(1)}, f32[1,128]{1,0:T(1,128)S(1)}) %tuple.93, ...), branch_computations={%region_13.14_spmd, %region_14.15_spmd, %region_15.16_spmd, %regio... | conditional | flops 76800 | bytes 14985936 | solution.py:231
  70.1 0.1 pad.20.clone
  70.2 0.1 maximum_maximum_fusion
  70.3 0.1 broadcast_in_dim.24
  70.4 18.8 %all_to_all.50.mine = f32[16,136,128]{2,1,0:T(8,128)S(1)} all-to-all(f32[16,136,128]{2,1,0:T(8,128)S(1)} %broadcast_in_dim.24), channel_id=1, replica_groups=mesh['q'=16,'c'=2,'z'=16] {'q'}, dimensions={0} | all-to-all | bytes 2228224 | tf_op jit(solution)/shard_map/cond/branch_0_fun/all_to_all | solution.py:26
  89.1 5.2 %collective-permute-start.1 = (f32[16,136,128]{2,1,0:T(8,128)S(1)}, f32[16,136,128]{2,1,0:T(8,128)S(1)}, u32[]{:S(2)}, u32[]{:S(2)}) collective-permute-start(f32[16,136,128]{2,1,0:T(8,128)S(1)} %all_to_all.50.mine), channel_id=1, source_target_pairs={{0,16},{16,0},{1,17},{17,1},{2,18},{18,2},{3,19},{19,3},{4,20},{20... | collective-permute-start | bytes 3342344 | tf_op jit(solution)/shard_map/cond/branch_0_fun/ppermute | solution.py:196
  94.3 1.9 %collective-permute-start.2 = (f32[16,128,128]{2,1,0:T(8,128)S(1)}, f32[16,128,128]{2,1,0:T(8,128)S(1)}, u32[]{:S(2)}, u32[]{:S(2)}) collective-permute-start(f32[16,128,128]{2,1,0:T(8,128)S(1)} %get-tuple-element.59.own), channel_id=1, source_target_pairs={{0,16},{16,0},{1,17},{17,1},{2,18},{18,2},{3,19},{19,3},{4,20},{20... | collective-permute-start | bytes 3145736 | tf_op jit(solution)/shard_map/cond/branch_0_fun/ppermute | solution.py:193
  96.3 2.6 %collective-permute-done.2.others = f32[16,128,128]{2,1,0:T(8,128)S(1)} collective-permute-done((f32[16,128,128]{2,1,0:T(8,128)S(1)}, f32[16,128,128]{2,1,0:T(8,128)S(1)}, u32[]{:S(2)}, u32[]{:S(2)}) %collective-permute-start.2) | collective-permute-done | bytes 1048608 | tf_op jit(solution)/shard_map/cond/branch_0_fun/ppermute | solution.py:193
  98.9 0.0 collective-permute-done.1.other
  98.9 2.2 %finish.3 = (f32[16,2,128,128]{3,2,1,0:T(8,128)}, f32[128,128]{1,0:T(8,128)}, f32[1,1]{1,0:T(1,128)}, f32[1,128]{1,0:T(1,128)}) custom-call(f32[16,136,128]{2,1,0:T(8,128)S(1)} %all_to_all.50.mine, f32[16,136,128]{2,1,0:T(8,128)S(1)} %collective-permute-done.1.other, f32[16,128,128]{2,1,0:T(8,128)S(1)} %get-tuple-element.59.own, ...), custom_call_target="tpu_custom_call" | custom-call | tf_op jit(solution)/shard_map/cond/branch_0_fun/finish/pallas_call | solution.py:154
  (10 shorter events, 0.1 us)
Async XLA Ops:
  0.6 1.2 %copy-start = (bf16[1,4096,128]{2,1,0:T(8,128)(2,1)S(1)}, bf16[1,4096,128]{2,1,0:T(8,128)(2,1)}, u32[]{:S(2)}) copy-start(bf16[1,4096,128]{2,1,0:T(8,128)(2,1)} %param.12) | copy-start | bytes 3145732
  1.9 9.2 %copy-start.1 = (bf16[1,4096,128]{2,1,0:T(8,128)(2,1)S(1)}, bf16[1,4096,128]{2,1,0:T(8,128)(2,1)}, u32[]{:S(2)}) copy-start(bf16[1,4096,128]{2,1,0:T(8,128)(2,1)} %param.12) | copy-start | bytes 3145732
  2.1 11.2 %collective-permute-start.7 = (f32[16,128,128]{2,1,0:T(8,128)S(1)}, f32[16,128,128]{2,1,0:T(8,128)S(1)}, u32[]{:S(2)}, u32[]{:S(2)}) collective-permute-start(f32[16,128,128]{2,1,0:T(8,128)S(1)} %sent_rows.1), channel_id=1, source_target_pairs={{0,16},{16,0},{1,17},{17,1},{2,18},{18,2},{3,19},{19,3},{4,20},{20... | collective-permute-start | bytes 3145736 | tf_op jit(solution)/shard_map/ppermute | solution.py:212
  11.2 2.3 %copy-start.2 = (f32[128,128]{1,0:T(8,128)S(1)}, f32[128,128]{1,0:T(8,128)}, u32[]{:S(2)}) copy-start(f32[128,128]{1,0:T(8,128)} %param.13) | copy-start | bytes 196612
  13.5 42.5 %copy-start.5 = (f32[128]{0:T(128)S(1)}, f32[128]{0:T(128)}, u32[]{:S(2)}) copy-start(f32[128]{0:T(128)} %param.15) | copy-start | bytes 1540
  13.5 56.5 %copy-start.4 = (f32[128]{0:T(128)S(1)}, f32[128]{0:T(128)}, u32[]{:S(2)}) copy-start(f32[128]{0:T(128)} %param.14) | copy-start | bytes 1540
  56.0 14.1 %copy-start.3 = (f32[128]{0:T(128)}, f32[128]{0:T(128)S(1)}, u32[]{:S(2)}) copy-start(f32[128]{0:T(128)S(1)} %get-tuple-element.134) | copy-start | bytes 1540
  89.1 9.7 %collective-permute-start.1 = (f32[16,136,128]{2,1,0:T(8,128)S(1)}, f32[16,136,128]{2,1,0:T(8,128)S(1)}, u32[]{:S(2)}, u32[]{:S(2)}) collective-permute-start(f32[16,136,128]{2,1,0:T(8,128)S(1)} %all_to_all.50.mine), channel_id=1, source_target_pairs={{0,16},{16,0},{1,17},{17,1},{2,18},{18,2},{3,19},{19,3},{4,20},{20... | collective-permute-start | bytes 3342344 | tf_op jit(solution)/shard_map/cond/branch_0_fun/ppermute | solution.py:196
  94.3 4.6 %collective-permute-start.2 = (f32[16,128,128]{2,1,0:T(8,128)S(1)}, f32[16,128,128]{2,1,0:T(8,128)S(1)}, u32[]{:S(2)}, u32[]{:S(2)}) collective-permute-start(f32[16,128,128]{2,1,0:T(8,128)S(1)} %get-tuple-element.59.own), channel_id=1, source_target_pairs={{0,16},{16,0},{1,17},{17,1},{2,18},{18,2},{3,19},{19,3},{4,20},{20... | collective-permute-start | bytes 3145736 | tf_op jit(solution)/shard_map/cond/branch_0_fun/ppermute | solution.py:193

commit v4 on v3

v4 whole, which is shorter than its diff:
```python
import functools

import jax
import jax.numpy as jnp
from jax import lax
from jax.experimental import pallas as pl
from jax.experimental.pallas import tpu as pltpu
from jax.sharding import Mesh, PartitionSpec as P

D = 4096
STEP = 10
FLAT = 2048
Q, C, Z = 16, 2, 16
ROWS = D // (Q * C)
COLS = FLAT // Z
AHEAD = (128, 112, 96, 72, 64, 0)
DP = ("q", "c")
SWAP = [(0, 1), (1, 0)]
VMEM = pl.BlockSpec(memory_space=pltpu.VMEM)
HBM = pl.BlockSpec(memory_space=pltpu.HBM)
ANY = pl.BlockSpec(memory_space=pl.ANY)


def share(x, axes, n):
    return lax.all_to_all(
        jnp.broadcast_to(x[None], (n, *x.shape)), axes, 0, 0, tiled=True
    )


def clip(ones, others):
    one, other = ones[0], others[0]
    for i in range(1, Q):
        one, other = one + ones[i], other + others[i]
    totals = jnp.sum(one + other, 1, keepdims=True)
    row_mean = totals[0:1] / D
    rms_value = jnp.sqrt(row_mean * totals[1:2] / (D * FLAT))
    return rms_value, jnp.sqrt(row_mean) / jnp.maximum(1.0, rms_value)


def step_body(parts, scaled, weights, update, stepped, rms):
    rms_value, gain = clip(
        [parts[C * i] for i in range(Q)], [parts[C * i + 1] for i in range(Q)]
    )
    new = scaled[...] * gain
    update[...] = new
    after = weights[...] - 0.001 * new
    for i in range(Q):
        stepped[i] = after
    rms[...] = rms_value


def step(parts, scaled, weights):
    return pl.pallas_call(
        step_body,
        out_shape=(
            jax.ShapeDtypeStruct((ROWS, COLS), jnp.float32),
            jax.ShapeDtypeStruct((Q, ROWS, COLS), jnp.float32),
            jax.ShapeDtypeStruct((1, 1), jnp.float32),
        ),
        in_specs=[VMEM, VMEM, VMEM],
        out_specs=(VMEM, VMEM, VMEM),
        compiler_params=pltpu.CompilerParams(vmem_limit_bytes=16 * 2**20),
        name="step",
    )(parts, scaled, weights)


def copy_all(pairs, sems):
    copies = [
        pltpu.make_async_copy(source, target, sems.at[i])
        for i, (source, target) in enumerate(pairs)
    ]
    for copy in copies:
        copy.start()
    for copy in copies:
        copy.wait()


def small_body(new, rms, row, update, rms_out, row_out, sems):
    copy_all([(new, update), (rms, rms_out), (row, row_out)], sems)


def small(new, rms, row):
    return pl.pallas_call(
        small_body,
        out_shape=(
            jax.ShapeDtypeStruct((ROWS, COLS), jnp.float32),
            jax.ShapeDtypeStruct((1, 1), jnp.float32),
            jax.ShapeDtypeStruct((1, ROWS), jnp.float32),
        ),
        in_specs=[ANY] * 3,
        out_specs=(HBM,) * 3,
        scratch_shapes=[pltpu.SemaphoreType.DMA((3,))],
        compiler_params=pltpu.CompilerParams(vmem_limit_bytes=16 * 2**20),
        cost_estimate=pl.CostEstimate(
            flops=0, bytes_accessed=Q * ROWS * COLS * 4, transcendentals=0
        ),
        name="small",
    )(new, rms, row)


def lay_body(mine, other, whole, sems):
    core = lax.axis_index("c")
    copy_all([(mine, whole.at[:, core]), (other, whole.at[:, 1 - core])], sems)


def lay(mine, other):
    return pl.pallas_call(
        lay_body,
        out_shape=jax.ShapeDtypeStruct((Q, C, ROWS, COLS), jnp.float32),
        in_specs=[ANY] * 2,
        out_specs=HBM,
        scratch_shapes=[pltpu.SemaphoreType.DMA((2,))],
        compiler_params=pltpu.CompilerParams(vmem_limit_bytes=16 * 2**20),
        name="lay",
    )(mine, other)


def finish_body(ahead, mine, other, own, others, scaled, row, *refs):
    whole, update, rms, row_out = refs
    core = lax.axis_index("c")
    tail = pl.ds(ROWS, 8)
    rms_value, gain = clip(
        [mine[i, tail][0:2] for i in range(Q)], [other[i, tail][0:2] for i in range(Q)]
    )
    rms[...] = rms_value
    update[...] = scaled[...] * gain
    row_out[...] = row[...]
    lowered = 0.001 * gain
    for j in range(Q):
        for side, rows, known in ((core, mine, own), (1 - core, other, others)):
            whole[j, side, :ahead] = known[j] - lowered * rows[j, :ahead]
            if ahead < ROWS:
                whole[j, side, ahead:] = (
                    rows[j, ROWS + 8 :] - lowered * rows[j, ahead:ROWS]
                )


def finish(ahead, mine, other, own, others, scaled, row):
    whole = (Q, C, ROWS, COLS)
    return pl.pallas_call(
        functools.partial(finish_body, ahead),
        out_shape=(
            jax.ShapeDtypeStruct(whole, jnp.float32),
            jax.ShapeDtypeStruct((ROWS, COLS), jnp.float32),
            jax.ShapeDtypeStruct((1, 1), jnp.float32),
            jax.ShapeDtypeStruct((1, ROWS), jnp.float32),
        ),
        in_specs=[VMEM] * 6,
        out_specs=(VMEM,) * 4,
        compiler_params=pltpu.CompilerParams(vmem_limit_bytes=16 * 2**20),
        name="finish",
    )(mine, other, own, others, scaled, row)


def front(ahead, chip, weights):
    sent = chip
    if ahead:
        rows = jnp.broadcast_to(weights[None, :ahead], (Q, ahead, COLS))
        sent = jnp.concatenate([chip, rows], 1)
    got = lax.all_to_all(sent, "q", 0, 0, tiled=True)
    rows = jnp.pad(got[:, ROWS:], ((0, 0), (0, ROWS - ahead), (0, 0)))
    return jnp.sum(got[:, :ROWS], 0) / (Q * C), rows


def back(ahead, scaled, parts, row, weights, own_weights):
    if ahead:
        outs = back_early(ahead, scaled, parts, row, weights, own_weights)
    else:
        outs = back_late(scaled, parts, row, weights)
    return outs[0].reshape(D, COLS), outs[1], outs[2].reshape(()), outs[3][0]


def back_early(ahead, scaled, parts, row, weights, own_weights):
    own = own_weights[:, :ahead]
    others = lax.ppermute(own, "c", SWAP)
    empty = jnp.zeros((6, COLS), jnp.float32)
    mine = share(jnp.concatenate([scaled, parts, empty, weights[ahead:]]), "q", Q)
    other = lax.ppermute(mine, "c", SWAP)
    return finish(ahead, mine, other, own, others, scaled, row)


def back_late(scaled, parts, row, weights):
    parts = share(parts, DP, Q * C)
    new, stepped, rms = step(parts, scaled, weights)
    mine = lax.all_to_all(stepped, "q", 0, 0, tiled=True)
    mine, new, rms, row = lax.optimization_barrier((mine, new, rms, row))
    other = lax.ppermute(mine, "c", SWAP)
    update, rms, row = small(new, rms, row)
    return lay(mine, other), update, rms, row


def per_device(replica_grads, weights, row_state, col_state):
    decay_rate = 1.0 - float(STEP) ** (-0.8)

    grads = replica_grads.reshape(Q, C, ROWS, COLS)
    core = lax.axis_index("c")
    sent = lax.dynamic_index_in_dim(grads, 1 - core, 1, False).astype(jnp.float32)
    sent, grads = lax.optimization_barrier((sent, grads))
    other = lax.ppermute(sent, "c", SWAP)
    kept = lax.dynamic_index_in_dim(grads, core, 1, False)
    kept = lax.optimization_barrier(kept.astype(jnp.float32))
    chip = kept + other
    plane = jnp.clip(lax.axis_index("z") - 1, 0, len(AHEAD) - 1)
    mean_grad, own_weights = lax.switch(
        plane, [functools.partial(front, n) for n in AHEAD], chip, weights
    )

    square = mean_grad * mean_grad + 1e-30
    col_sums = jnp.sum(share(jnp.sum(square, 0)[None], DP, Q * C), (0, 1))
    col_new = decay_rate * col_state + (1.0 - decay_rate) * (col_sums / D)
    both = jnp.stack(
        [jnp.sum(square, 1), jnp.sum(mean_grad * mean_grad * (1.0 / col_new), 1)]
    )
    both = jnp.sum(share(both, "z", Z), 0)
    row_new = decay_rate * row_state + (1.0 - decay_rate) * (both[0] / FLAT)
    scaled = mean_grad * lax.rsqrt(row_new[:, None] * col_new[None, :])
    parts = jnp.stack([row_new, both[1] / row_new])
    new_weights, update, rms_value, row_new = lax.switch(
        plane,
        [functools.partial(back, n) for n in AHEAD],
        *(scaled, parts, row_new[None], weights, own_weights),
    )
    return (new_weights, update, row_new, col_new, rms_value)


def solution(mesh):
    split_mesh = Mesh(mesh.devices.reshape(Q, C, Z), ("q", "c", "z"))
    in_specs = (P(DP, None, "z"), P(DP, "z"), P(DP), P("z"))
    out_specs = (P(None, "z"), P(DP, "z"), P(DP), P("z"), P())
    return jax.shard_map(
        per_device,
        mesh=split_mesh,
        in_specs=in_specs,
        out_specs=out_specs,
        check_vma=False,
    )
```

time: 101 us -> 101 us (level)
  Pallas kernels: 2.45 us -> 0.94 us
  other arithmetic: 0.99 us -> 2.22 us
    pallas_call x1, Pallas kernels: 2.18 us -> 0.94 us  [finish(): pl.pallas_call(functools.partial(finish_body, ahead), out_shape=(jax.Shap...]
    convert_element_type x0 -> x1, other arithmetic: none -> 1.23 us  [per_device(): lax.dynamic_index_in_dim(grads, 1 - core, 1, False).astype(jnp.float32)]
where the time goes in v4:
time: 101 us
  blocking collectives  74.4 us (74%)
  starting transfers between devices  15.9 us (16%)
  waiting for transfers between devices  4.75 us (5%)
  other arithmetic  2.22 us (2%)
  local copies, waits for them, and re-layouts  1.61 us (2%)
    all_to_all x3, blocking collectives, share(): lax.all_to_all(jnp.broadcast_to(x[None], (n, *x.shape)), axes, 0, 0, tile...  43.8 us
    all_to_all x1, blocking collectives, front(): got = lax.all_to_all(sent, 'q', 0, 0, tiled=True)  30.6 us
    ppermute x1, starting transfers between devices, per_device(): other = lax.ppermute(sent, 'c', SWAP)  8.79 us
    ppermute x1, starting transfers between devices, back_early(): other = lax.ppermute(mine, 'c', SWAP)  5.18 us
    ppermute x1, waiting for transfers between devices, back_early(): others = lax.ppermute(own, 'c', SWAP)  2.63 us
    ppermute x1, waiting for transfers between devices, per_device(): other = lax.ppermute(sent, 'c', SWAP)  2.12 us
  transfers between devices with their start and end apart: 3, of which 2 were waited for; matrix products, arithmetic and copies ran while one was open for 0% of the time, Pallas kernels for 0%

profile of v4, /device:TPU:1, one launch (start us, length us, event | category | flops | bytes accessed | tf_op | source)
XLA Modules:
  0.0 100.7 jit_solution(9703216008612030981)
XLA Ops:
  0.6 0.0 copy-start.1
  0.6 1.2 %bitcast_convert_fusion = f32[16,128,128]{2,1,0:T(8,128)S(1)} fusion(bf16[16,2,128,128]{3,2,1,0:T(8,128)(2,1)} %bitcast.25, s32[]{:T(128)S(6)} %select_n.7), kind=kLoop, calls=%fused_computation.21 | loop fusion | flops 262144 | bytes 1572868 | tf_op jit(solution)/shard_map/convert_element_type | solution.py:197
  1.9 8.8 %collective-permute-start.11 = (f32[16,128,128]{2,1,0:T(8,128)S(1)}, f32[16,128,128]{2,1,0:T(8,128)S(1)}, u32[]{:S(2)}, u32[]{:S(2)}) collective-permute-start(f32[16,128,128]{2,1,0:T(8,128)S(1)} %bitcast_convert_fusion), channel_id=1, source_target_pairs={{0,16},{16,0},{1,17},{17,1},{2,18},{18,2},{3,19},{19,3},{4,20},{20... | collective-permute-start | bytes 3145736 | tf_op jit(solution)/shard_map/ppermute | solution.py:199
  10.7 0.0 copy-done.1
  10.7 0.1 bitcast_convert_fusion.1
  10.8 0.0 copy-start
  10.8 2.1 %collective-permute-done.11 = f32[16,128,128]{2,1,0:T(8,128)S(1)} collective-permute-done((f32[16,128,128]{2,1,0:T(8,128)S(1)}, f32[16,128,128]{2,1,0:T(8,128)S(1)}, u32[]{:S(2)}, u32[]{:S(2)}) %collective-permute-start.11) | collective-permute-done | bytes 1048608 | tf_op jit(solution)/shard_map/ppermute | solution.py:199
  12.9 0.1 add.37
  13.1 0.0 copy-done
  13.1 0.0 copy-start.4
  13.1 0.0 copy-start.3
  13.1 31.1 %conditional.2 = (f32[128,128]{1,0:T(8,128)S(1)}, f32[16,128,128]{2,1,0:T(8,128)S(1)}, f32[128,128]{1,0:T(8,128)S(1)}) conditional(s32[]{:T(128)} %clamp.4, (f32[128,128]{1,0:T(8,128)S(1)}, f32[16,128,128]{2,1,0:T(8,128)S(1)}) %tuple.99, (f32[128,128]{1,0:T(8,128)S(1)}, f32[16,128,128]{2,1,0:T(8,128)S(1)}) %tuple.100, ...), branch_computations={%region_0.2_spmd, %region_2.4_spmd, %region_4.6_spmd, %region_6.8_... | conditional | flops 802816 | bytes 14065692 | solution.py:204
  13.1 0.1 broadcast_in_dim.18
  13.2 0.2 pad_maximum_fusion
  13.4 30.6 %all_to_all.62 = f32[16,256,128]{2,1,0:T(8,128)S(1)} all-to-all(f32[16,256,128]{2,1,0:T(8,128)S(1)} %pad_maximum_fusion), channel_id=1, replica_groups=mesh['q'=16,'c'=2,'z'=16] {'q'}, dimensions={0} | all-to-all | bytes 4194304 | tf_op jit(solution)/shard_map/cond/branch_0_fun/all_to_all | solution.py:160
  44.0 0.1 fusion.7
  44.2 0.1 add_reduce_fusion.1
  44.3 11.3 %all_to_all.75 = f32[32,1,128]{2,1,0:T(1,128)S(1)} all-to-all(f32[32,1,128]{2,1,0:T(1,128)S(1)} %broadcast_in_dim.46), channel_id=1, replica_groups=mesh['q'=16,'c'=2,'z'=16] {'q','c'}, dimensions={0} | all-to-all | bytes 32768 | tf_op jit(solution)/shard_map/all_to_all | solution.py:25
  55.6 0.0 copy-done.4
  55.6 0.0 copy-start.2
  55.6 0.1 multiply_reduce_fusion
  55.7 13.8 %all_to_all.76 = f32[16,2,128]{2,1,0:T(2,128)S(1)} all-to-all(f32[16,2,128]{2,1,0:T(2,128)S(1)} %broadcast_in_dim.47), channel_id=1, replica_groups=mesh['q'=16,'c'=2,'z'=16] {'z'}, dimensions={0} | all-to-all | bytes 32768 | tf_op jit(solution)/shard_map/all_to_all | solution.py:25
  69.6 0.0 copy-done.3
  69.6 0.1 rsqrt_multiply_fusion
  69.7 0.0 copy-done.2
  69.7 29.7 %conditional.3 = (f32[128,128]{1,0:T(8,128)}, f32[16,2,128,128]{3,2,1,0:T(8,128)S(1)}, f32[1,1]{1,0:T(1,128)}, f32[1,128]{1,0:T(1,128)}) conditional(s32[]{:T(128)} %clamp.4, (f32[128,128]{1,0:T(8,128)S(1)}, f32[2,128]{1,0:T(2,128)S(1)}, f32[16,128,128]{2,1,0:T(8,128)S(1)}, f32[1,128]{1,0:T(1,128)S(1)}) %tuple.109, ...), branch_computations={%region_17.18_spmd, %region_18.19_spmd, %region_19.20_spmd, %regio... | conditional | flops 76800 | bytes 14985960 | solution.py:218
  69.7 0.1 pad.32.clone
  69.8 0.1 maximum_maximum_fusion
  69.9 0.1 broadcast_in_dim.34
  70.0 18.7 %all_to_all.68.mine = f32[16,136,128]{2,1,0:T(8,128)S(1)} all-to-all(f32[16,136,128]{2,1,0:T(8,128)S(1)} %broadcast_in_dim.34), channel_id=1, replica_groups=mesh['q'=16,'c'=2,'z'=16] {'q'}, dimensions={0} | all-to-all | bytes 2228224 | tf_op jit(solution)/shard_map/cond/branch_0_fun/all_to_all | solution.py:25
  88.7 5.2 %collective-permute-start.1 = (f32[16,136,128]{2,1,0:T(8,128)S(1)}, f32[16,136,128]{2,1,0:T(8,128)S(1)}, u32[]{:S(2)}, u32[]{:S(2)}) collective-permute-start(f32[16,136,128]{2,1,0:T(8,128)S(1)} %all_to_all.68.mine), channel_id=1, source_target_pairs={{0,16},{16,0},{1,17},{17,1},{2,18},{18,2},{3,19},{19,3},{4,20},{20... | collective-permute-start | bytes 3342344 | tf_op jit(solution)/shard_map/cond/branch_0_fun/ppermute | solution.py:178
  93.9 1.9 %collective-permute-start.2 = (f32[16,128,128]{2,1,0:T(8,128)S(1)}, f32[16,128,128]{2,1,0:T(8,128)S(1)}, u32[]{:S(2)}, u32[]{:S(2)}) collective-permute-start(f32[16,128,128]{2,1,0:T(8,128)S(1)} %get-tuple-element.94.own), channel_id=1, source_target_pairs={{0,16},{16,0},{1,17},{17,1},{2,18},{18,2},{3,19},{19,3},{4,20},{20... | collective-permute-start | bytes 3145736 | tf_op jit(solution)/shard_map/cond/branch_0_fun/ppermute | solution.py:175
  95.8 2.6 %collective-permute-done.2.others = f32[16,128,128]{2,1,0:T(8,128)S(1)} collective-permute-done((f32[16,128,128]{2,1,0:T(8,128)S(1)}, f32[16,128,128]{2,1,0:T(8,128)S(1)}, u32[]{:S(2)}, u32[]{:S(2)}) %collective-permute-start.2) | collective-permute-done | bytes 1048608 | tf_op jit(solution)/shard_map/cond/branch_0_fun/ppermute | solution.py:175
  98.5 0.0 collective-permute-done.1.other
  98.5 0.9 finish.5
  99.4 0.0 copy-start.5
  99.4 1.3 %copy-done.5 = f32[16,2,128,128]{3,2,1,0:T(8,128)} copy-done((f32[16,2,128,128]{3,2,1,0:T(8,128)}, f32[16,2,128,128]{3,2,1,0:T(8,128)S(1)}, u32[]{:S(2)}) %copy-start.5) | copy-done | bytes 2097176
  (10 shorter events, 0.1 us)
Async XLA Ops:
  0.6 10.1 %copy-start.1 = (bf16[1,4096,128]{2,1,0:T(8,128)(2,1)S(1)}, bf16[1,4096,128]{2,1,0:T(8,128)(2,1)}, u32[]{:S(2)}) copy-start(bf16[1,4096,128]{2,1,0:T(8,128)(2,1)} %param.16) | copy-start | bytes 3145732
  1.9 11.1 %collective-permute-start.11 = (f32[16,128,128]{2,1,0:T(8,128)S(1)}, f32[16,128,128]{2,1,0:T(8,128)S(1)}, u32[]{:S(2)}, u32[]{:S(2)}) collective-permute-start(f32[16,128,128]{2,1,0:T(8,128)S(1)} %bitcast_convert_fusion), channel_id=1, source_target_pairs={{0,16},{16,0},{1,17},{17,1},{2,18},{18,2},{3,19},{19,3},{4,20},{20... | collective-permute-start | bytes 3145736 | tf_op jit(solution)/shard_map/ppermute | solution.py:199
  10.8 2.3 %copy-start = (f32[128,128]{1,0:T(8,128)S(1)}, f32[128,128]{1,0:T(8,128)}, u32[]{:S(2)}) copy-start(f32[128,128]{1,0:T(8,128)} %param.17) | copy-start | bytes 196612
  13.1 42.5 %copy-start.4 = (f32[128]{0:T(128)S(1)}, f32[128]{0:T(128)}, u32[]{:S(2)}) copy-start(f32[128]{0:T(128)} %param.19) | copy-start | bytes 1540
  13.1 56.5 %copy-start.3 = (f32[128]{0:T(128)S(1)}, f32[128]{0:T(128)}, u32[]{:S(2)}) copy-start(f32[128]{0:T(128)} %param.18) | copy-start | bytes 1540
  55.6 14.1 %copy-start.2 = (f32[128]{0:T(128)}, f32[128]{0:T(128)S(1)}, u32[]{:S(2)}) copy-start(f32[128]{0:T(128)S(1)} %get-tuple-element.190) | copy-start | bytes 1540
  88.7 9.7 %collective-permute-start.1 = (f32[16,136,128]{2,1,0:T(8,128)S(1)}, f32[16,136,128]{2,1,0:T(8,128)S(1)}, u32[]{:S(2)}, u32[]{:S(2)}) collective-permute-start(f32[16,136,128]{2,1,0:T(8,128)S(1)} %all_to_all.68.mine), channel_id=1, source_target_pairs={{0,16},{16,0},{1,17},{17,1},{2,18},{18,2},{3,19},{19,3},{4,20},{20... | collective-permute-start | bytes 3342344 | tf_op jit(solution)/shard_map/cond/branch_0_fun/ppermute | solution.py:178
  93.9 4.6 %collective-permute-start.2 = (f32[16,128,128]{2,1,0:T(8,128)S(1)}, f32[16,128,128]{2,1,0:T(8,128)S(1)}, u32[]{:S(2)}, u32[]{:S(2)}) collective-permute-start(f32[16,128,128]{2,1,0:T(8,128)S(1)} %get-tuple-element.94.own), channel_id=1, source_target_pairs={{0,16},{16,0},{1,17},{17,1},{2,18},{18,2},{3,19},{19,3},{4,20},{20... | collective-permute-start | bytes 3145736 | tf_op jit(solution)/shard_map/cond/branch_0_fun/ppermute | solution.py:175
  99.4 1.3 %copy-start.5 = (f32[16,2,128,128]{3,2,1,0:T(8,128)}, f32[16,2,128,128]{3,2,1,0:T(8,128)S(1)}, u32[]{:S(2)}) copy-start(f32[16,2,128,128]{3,2,1,0:T(8,128)S(1)} %get-tuple-element.169) | copy-start | bytes 6291460

commit v5 on v4

--- a/solution.py
+++ b/solution.py
@@ -13,7 +13,12 @@
 Q, C, Z = 16, 2, 16
 ROWS = D // (Q * C)
 COLS = FLAT // Z
-AHEAD = (128, 112, 96, 72, 64, 0)
+AHEAD = (128, 112, 80, 56, 0)
+SIDE = range(4)
+ALONG_X = [[[(y * 4 + x) * C + c for x in SIDE] for y in SIDE] for c in range(C)]
+ALONG_Y = [[[(y * 4 + x) * C + c for y in SIDE] for x in SIDE] for c in range(C)]
+FIRST = ALONG_X[0] + ALONG_Y[1]
+SECOND = ALONG_Y[0] + ALONG_X[1]
 DP = ("q", "c")
 SWAP = [(0, 1), (1, 0)]
 VMEM = pl.BlockSpec(memory_space=pltpu.VMEM)
@@ -128,7 +133,8 @@
     lowered = 0.001 * gain
     for j in range(Q):
         for side, rows, known in ((core, mine, own), (1 - core, other, others)):
-            whole[j, side, :ahead] = known[j] - lowered * rows[j, :ahead]
+            at = jnp.where(side == 0, j, j % 4 * 4 + j // 4)
+            whole[j, side, :ahead] = known[at, :ahead] - lowered * rows[j, :ahead]
             if ahead < ROWS:
                 whole[j, side, ahead:] = (
                     rows[j, ROWS + 8 :] - lowered * rows[j, ahead:ROWS]
@@ -152,27 +158,68 @@
     )(mine, other, own, others, scaled, row)
 
 
-def front(ahead, chip, weights):
-    sent = chip
+def arrange_body(ahead, kept, other, weights, out):
+    turn = lax.axis_index("c") == 0
+    for i in range(4):
+        for j in range(4):
+            at = jnp.where(turn, j * 4 + i, i * 4 + j)
+            out[i, j * ROWS : (j + 1) * ROWS] = kept[at] + other[at]
+        out[i, 4 * ROWS :] = weights[:ahead]
+
+
+def arrange(ahead, kept, other, weights):
+    return pl.pallas_call(
+        functools.partial(arrange_body, ahead),
+        out_shape=jax.ShapeDtypeStruct((4, 4 * ROWS + ahead, COLS), jnp.float32),
+        in_specs=[VMEM] * 3,
+        out_specs=VMEM,
+        compiler_params=pltpu.CompilerParams(vmem_limit_bytes=16 * 2**20),
+        name="arrange",
+    )(kept, other, weights)
+
+
+def column_sums(mean_grad):
+    square = mean_grad * mean_grad + 1e-30
+    return jnp.sum(share(jnp.sum(square, 0)[None], DP, Q * C), (0, 1))
+
+
+def front(ahead, kept, other, weights):
+    if not ahead:
+        got = lax.all_to_all(kept + other, "q", 0, 0, tiled=True)
+        mean_grad = jnp.sum(got, 0) / (Q * C)
+        none = jnp.zeros((Q, ROWS, COLS), jnp.float32)
+        return mean_grad, column_sums(mean_grad), none, none
+
+    def exchange(x, groups):
+        return lax.all_to_all(x, DP, 0, 0, axis_index_groups=groups, tiled=True)
+
+    got = exchange(arrange(ahead, kept, other, weights), FIRST)
+    sums = jnp.sum(got[:, : 4 * ROWS], 0).reshape(4, ROWS, COLS)
+    rows = got[:, 4 * ROWS :].reshape(1, 4 * ahead, COLS)
+    rows = jnp.broadcast_to(rows, (4, 4 * ahead, COLS))
+    got = exchange(jnp.concatenate([sums, rows], 1), SECOND)
+    mean_grad = jnp.sum(got[:, :ROWS], 0) / (Q * C)
+    rows = got[:, ROWS:].reshape(Q, ahead, COLS)
+    if ahead < ROWS:
+        rows = jnp.pad(rows, ((0, 0), (0, ROWS - ahead), (0, 0)))
+        others = jnp.zeros_like(rows)
+    else:
+        others = lax.ppermute(rows, "c", SWAP)
+    return mean_grad, column_sums(mean_grad), rows, others
+
+
+def back(ahead, scaled, parts, row, weights, own, others):
     if ahead:
-        rows = jnp.broadcast_to(weights[None, :ahead], (Q, ahead, COLS))
-        sent = jnp.concatenate([chip, rows], 1)
-    got = lax.all_to_all(sent, "q", 0, 0, tiled=True)
-    rows = jnp.pad(got[:, ROWS:], ((0, 0), (0, ROWS - ahead), (0, 0)))
-    return jnp.sum(got[:, :ROWS], 0) / (Q * C), rows
-
-
-def back(ahead, scaled, parts, row, weights, own_weights):
-    if ahead:
-        outs = back_early(ahead, scaled, parts, row, weights, own_weights)
+        outs = back_early(ahead, scaled, parts, row, weights, own, others)
     else:
         outs = back_late(scaled, parts, row, weights)
     return outs[0].reshape(D, COLS), outs[1], outs[2].reshape(()), outs[3][0]
 
 
-def back_early(ahead, scaled, parts, row, weights, own_weights):
-    own = own_weights[:, :ahead]
-    others = lax.ppermute(own, "c", SWAP)
+def back_early(ahead, scaled, parts, row, weights, own, others):
+    if ahead < ROWS:
+        own = own[:, :ahead]
+        others = lax.ppermute(own, "c", SWAP)
     empty = jnp.zeros((6, COLS), jnp.float32)
     mine = share(jnp.concatenate([scaled, parts, empty, weights[ahead:]]), "q", Q)
     other = lax.ppermute(mine, "c", SWAP)
@@ -199,14 +246,12 @@
     other = lax.ppermute(sent, "c", SWAP)
     kept = lax.dynamic_index_in_dim(grads, core, 1, False)
     kept = lax.optimization_barrier(kept.astype(jnp.float32))
-    chip = kept + other
-    plane = jnp.clip(lax.axis_index("z") - 1, 0, len(AHEAD) - 1)
-    mean_grad, own_weights = lax.switch(
-        plane, [functools.partial(front, n) for n in AHEAD], chip, weights
+    plane = jnp.clip(lax.axis_index("z") - 2, 0, len(AHEAD) - 1)
+    mean_grad, col_sums, own, others = lax.switch(
+        plane, [functools.partial(front, n) for n in AHEAD], kept, other, weights
     )
 
     square = mean_grad * mean_grad + 1e-30
-    col_sums = jnp.sum(share(jnp.sum(square, 0)[None], DP, Q * C), (0, 1))
     col_new = decay_rate * col_state + (1.0 - decay_rate) * (col_sums / D)
     both = jnp.stack(
         [jnp.sum(square, 1), jnp.sum(mean_grad * mean_grad * (1.0 / col_new), 1)]
@@ -218,7 +263,7 @@
     new_weights, update, rms_value, row_new = lax.switch(
         plane,
         [functools.partial(back, n) for n in AHEAD],
-        *(scaled, parts, row_new[None], weights, own_weights),
+        *(scaled, parts, row_new[None], weights, own, others),
     )
     return (new_weights, update, row_new, col_new, rms_value)
 

time: 101 us -> 101 us (level); the launches traced: 101 us -> 99.5 us
  blocking collectives: 74.4 us -> 71.6 us
  starting transfers between devices: 15.9 us -> 18 us
    all_to_all x1 -> x2, blocking collectives: 30.6 us -> 27.8 us  [exchange(): return lax.all_to_all(x, DP, 0, 0, axis_index_groups=groups, tiled=True)]
    ppermute x1, waiting for transfers between devices: 2.63 us -> 0.01 us  [front(): others = lax.ppermute(rows, 'c', SWAP)]
    ppermute x1, waiting for transfers between devices: 0.01 us -> 2.36 us  [back_early(): other = lax.ppermute(mine, 'c', SWAP)]
    ppermute x1, starting transfers between devices: 1.92 us -> 3.99 us  [front(): others = lax.ppermute(rows, 'c', SWAP)]
where the time goes in v5:
time: 101 us; the launch traced here: 99.5 us
  blocking collectives  71.6 us (71%)
  starting transfers between devices  18 us (18%)
  waiting for transfers between devices  4.5 us (4%)
  other arithmetic  1.88 us (2%)
  local copies, waits for them, and re-layouts  1.67 us (2%)
  Pallas kernels  1.06 us (1%)
    all_to_all x3, blocking collectives, share(): lax.all_to_all(jnp.broadcast_to(x[None], (n, *x.shape)), axes, 0, 0, tile...  43.8 us
    all_to_all x2, blocking collectives, exchange(): return lax.all_to_all(x, DP, 0, 0, axis_index_groups=groups, tiled=True)  27.8 us
    ppermute x1, starting transfers between devices, per_device(): other = lax.ppermute(sent, 'c', SWAP)  8.79 us
    ppermute x1, starting transfers between devices, back_early(): other = lax.ppermute(mine, 'c', SWAP)  5.18 us
    ppermute x1, starting transfers between devices, front(): others = lax.ppermute(rows, 'c', SWAP)  3.99 us
    ppermute x1, waiting for transfers between devices, back_early(): other = lax.ppermute(mine, 'c', SWAP)  2.36 us
    ppermute x1, waiting for transfers between devices, per_device(): other = lax.ppermute(sent, 'c', SWAP)  2.14 us
  transfers between devices with their start and end apart: 3, of which 2 were waited for; matrix products, arithmetic and copies ran while one was open for 0% of the time, Pallas kernels for 0%

profile of v5, /device:TPU:1, one launch (start us, length us, event | category | flops | bytes accessed | tf_op | source)
XLA Modules:
  0.0 99.5 jit_solution(9035091399969938084)
XLA Ops:
  0.6 0.0 copy-start.1
  0.6 0.0 copy-start
  0.7 1.2 %bitcast_convert_fusion.1 = f32[16,128,128]{2,1,0:T(8,128)S(1)} fusion(bf16[16,2,128,128]{3,2,1,0:T(8,128)(2,1)} %bitcast.48, s32[]{:T(128)S(6)} %select_n.7), kind=kLoop, calls=%fused_computation.27 | loop fusion | flops 262144 | bytes 1572868 | tf_op jit(solution)/shard_map/convert_element_type | solution.py:244
  1.9 8.8 %collective-permute-start.9 = (f32[16,128,128]{2,1,0:T(8,128)S(1)}, f32[16,128,128]{2,1,0:T(8,128)S(1)}, u32[]{:S(2)}, u32[]{:S(2)}) collective-permute-start(f32[16,128,128]{2,1,0:T(8,128)S(1)} %bitcast_convert_fusion.1), channel_id=1, source_target_pairs={{0,16},{16,0},{1,17},{17,1},{2,18},{18,2},{3,19},{19,3},{4,20},{20... | collective-permute-start | bytes 3145736 | tf_op jit(solution)/shard_map/ppermute | solution.py:246
  10.7 0.0 copy-done.1
  10.7 0.1 bitcast_convert_fusion
  10.8 2.1 %collective-permute-done.9 = f32[16,128,128]{2,1,0:T(8,128)S(1)} collective-permute-done((f32[16,128,128]{2,1,0:T(8,128)S(1)}, f32[16,128,128]{2,1,0:T(8,128)S(1)}, u32[]{:S(2)}, u32[]{:S(2)}) %collective-permute-start.9) | collective-permute-done | bytes 1048608 | tf_op jit(solution)/shard_map/ppermute | solution.py:246
  13.0 0.0 copy-done
  13.0 0.0 copy-start.4
  13.0 0.0 copy-start.3
  13.0 42.4 %conditional.2 = (f32[128,128]{1,0:T(8,128)S(1)}, f32[128]{0:T(128)S(1)}, f32[16,128,128]{2,1,0:T(8,128)S(1)}, f32[16,128,128]{2,1,0:T(8,128)S(1)}, f32[128,128]{1,0:T(8,128)S(1)}) conditional(s32[]{:T(128)} %clamp.4, (f32[16,128,128]{2,1,0:T(8,128)S(1)}, f32[16,128,128]{2,1,0:T(8,128)S(1)}, ...), branch_computations={%region_0.5_spmd, %region_5.10_spmd, %region_10.15_spmd, %region_1... | conditional | flops 642816 | bytes 17892948 | solution.py:250
  13.0 0.1 arrange.4
  13.1 13.9 %all_to_all.85 = f32[4,640,128]{2,1,0:T(8,128)S(1)} all-to-all(f32[4,640,128]{2,1,0:T(8,128)S(1)} %arrange.4), channel_id=1, replica_groups={{0,32,64,96},{128,160,192,224},{256,288,320,352},{384,416,448,480},{16,..., dimensions={0} | all-to-all | bytes 2621440 | tf_op jit(solution)/shard_map/cond/branch_0_fun/all_to_all | solution.py:194
  27.0 0.1 slice_reduce_fusion
  27.0 0.1 broadcast_in_dim.33
  27.1 0.1 pad_maximum_fusion
  27.2 13.9 %all_to_all.86 = f32[4,640,128]{2,1,0:T(8,128)S(1)} all-to-all(f32[4,640,128]{2,1,0:T(8,128)S(1)} %pad_maximum_fusion), channel_id=1, replica_groups={{0,128,256,384},{32,160,288,416},{64,192,320,448},{96,224,352,480},{16,..., dimensions={0} | all-to-all | bytes 2621440 | tf_op jit(solution)/shard_map/cond/branch_0_fun/all_to_all | solution.py:194
  41.1 0.1 slice.77
  41.2 4.0 %collective-permute-start.8 = (f32[16,128,128]{2,1,0:T(8,128)S(1)}, f32[16,128,128]{2,1,0:T(8,128)S(1)}, u32[]{:S(2)}, u32[]{:S(2)}) collective-permute-start(f32[16,128,128]{2,1,0:T(8,128)S(1)} %bitcast.39), channel_id=1, source_target_pairs={{0,16},{16,0},{1,17},{17,1},{2,18},{18,2},{3,19},{19,3},{4,20},{20... | collective-permute-start | bytes 3145736 | tf_op jit(solution)/shard_map/cond/branch_0_fun/ppermute | solution.py:207
  45.2 10.1 %all_to_all.87 = f32[32,1,128]{2,1,0:T(1,128)S(1)} all-to-all(f32[32,1,128]{2,1,0:T(1,128)S(1)} %broadcast_in_dim.42), channel_id=1, replica_groups=mesh['q'=16,'c'=2,'z'=16] {'q','c'}, dimensions={0} | all-to-all | bytes 32768 | tf_op jit(solution)/shard_map/cond/branch_0_fun/all_to_all | solution.py:30
  55.3 0.0 collective-permute-done.8
  55.3 0.0 copy-done.4
  55.3 0.0 copy-start.2
  55.4 0.1 add_reduce_fusion.5
  55.5 15.0 %all_to_all.100 = f32[16,2,128]{2,1,0:T(2,128)S(1)} all-to-all(f32[16,2,128]{2,1,0:T(2,128)S(1)} %broadcast_in_dim.70), channel_id=1, replica_groups=mesh['q'=16,'c'=2,'z'=16] {'z'}, dimensions={0} | all-to-all | bytes 32768 | tf_op jit(solution)/shard_map/all_to_all | solution.py:30
  70.5 0.0 copy-done.3
  70.5 0.1 rsqrt_multiply_fusion
  70.6 0.0 copy-done.2
  70.6 27.6 %conditional.3 = (f32[128,128]{1,0:T(8,128)}, f32[16,2,128,128]{3,2,1,0:T(8,128)S(1)}, f32[1,1]{1,0:T(1,128)}, f32[1,128]{1,0:T(1,128)}) conditional(s32[]{:T(128)} %clamp.4, (f32[128,128]{1,0:T(8,128)S(1)}, f32[2,128]{1,0:T(2,128)S(1)}, f32[16,128,128]{2,1,0:T(8,128)S(1)}, f32[16,128,128]{2,1,0:T(8,128)S(1)}, ...), branch_computations={%region_27.28_spmd, %region_28.29_spmd, %region_29.30_spmd, %regio... | conditional | flops 79872 | bytes 15072040 | solution.py:263
  70.7 0.1 pad.22.clone
  70.7 0.1 maximum_maximum_fusion
  70.8 0.1 broadcast_in_dim.64
  70.9 18.8 %all_to_all.94.mine = f32[16,136,128]{2,1,0:T(8,128)S(1)} all-to-all(f32[16,136,128]{2,1,0:T(8,128)S(1)} %broadcast_in_dim.64), channel_id=1, replica_groups=mesh['q'=16,'c'=2,'z'=16] {'q'}, dimensions={0} | all-to-all | bytes 2228224 | tf_op jit(solution)/shard_map/cond/branch_0_fun/all_to_all | solution.py:30
  89.7 5.2 %collective-permute-start.1 = (f32[16,136,128]{2,1,0:T(8,128)S(1)}, f32[16,136,128]{2,1,0:T(8,128)S(1)}, u32[]{:S(2)}, u32[]{:S(2)}) collective-permute-start(f32[16,136,128]{2,1,0:T(8,128)S(1)} %all_to_all.94.mine), channel_id=1, source_target_pairs={{0,16},{16,0},{1,17},{17,1},{2,18},{18,2},{3,19},{19,3},{4,20},{20... | collective-permute-start | bytes 3342344 | tf_op jit(solution)/shard_map/cond/branch_0_fun/ppermute | solution.py:225
  94.9 2.4 %collective-permute-done.1.other = f32[16,136,128]{2,1,0:T(8,128)S(1)} collective-permute-done((f32[16,136,128]{2,1,0:T(8,128)S(1)}, f32[16,136,128]{2,1,0:T(8,128)S(1)}, u32[]{:S(2)}, u32[]{:S(2)}) %collective-permute-start.1) | collective-permute-done | bytes 1114144 | tf_op jit(solution)/shard_map/cond/branch_0_fun/ppermute | solution.py:225
  97.3 0.9 finish.4
  98.2 0.0 copy-start.5
  98.2 1.3 %copy-done.5 = f32[16,2,128,128]{3,2,1,0:T(8,128)} copy-done((f32[16,2,128,128]{3,2,1,0:T(8,128)}, f32[16,2,128,128]{3,2,1,0:T(8,128)S(1)}, u32[]{:S(2)}) %copy-start.5) | copy-done | bytes 2097176
  (12 shorter events, 0.2 us)
Async XLA Ops:
  0.6 10.1 %copy-start.1 = (bf16[1,4096,128]{2,1,0:T(8,128)(2,1)S(1)}, bf16[1,4096,128]{2,1,0:T(8,128)(2,1)}, u32[]{:S(2)}) copy-start(bf16[1,4096,128]{2,1,0:T(8,128)(2,1)} %param.14) | copy-start | bytes 3145732
  0.6 12.3 %copy-start = (f32[128,128]{1,0:T(8,128)S(1)}, f32[128,128]{1,0:T(8,128)}, u32[]{:S(2)}) copy-start(f32[128,128]{1,0:T(8,128)} %param.15) | copy-start | bytes 196612
  1.9 11.1 %collective-permute-start.9 = (f32[16,128,128]{2,1,0:T(8,128)S(1)}, f32[16,128,128]{2,1,0:T(8,128)S(1)}, u32[]{:S(2)}, u32[]{:S(2)}) collective-permute-start(f32[16,128,128]{2,1,0:T(8,128)S(1)} %bitcast_convert_fusion.1), channel_id=1, source_target_pairs={{0,16},{16,0},{1,17},{17,1},{2,18},{18,2},{3,19},{19,3},{4,20},{20... | collective-permute-start | bytes 3145736 | tf_op jit(solution)/shard_map/ppermute | solution.py:246
  13.0 42.4 %copy-start.4 = (f32[128]{0:T(128)S(1)}, f32[128]{0:T(128)}, u32[]{:S(2)}) copy-start(f32[128]{0:T(128)} %param.17) | copy-start | bytes 1540
  13.0 57.6 %copy-start.3 = (f32[128]{0:T(128)S(1)}, f32[128]{0:T(128)}, u32[]{:S(2)}) copy-start(f32[128]{0:T(128)} %param.16) | copy-start | bytes 1540
  41.2 14.2 %collective-permute-start.8 = (f32[16,128,128]{2,1,0:T(8,128)S(1)}, f32[16,128,128]{2,1,0:T(8,128)S(1)}, u32[]{:S(2)}, u32[]{:S(2)}) collective-permute-start(f32[16,128,128]{2,1,0:T(8,128)S(1)} %bitcast.39), channel_id=1, source_target_pairs={{0,16},{16,0},{1,17},{17,1},{2,18},{18,2},{3,19},{19,3},{4,20},{20... | collective-permute-start | bytes 3145736 | tf_op jit(solution)/shard_map/cond/branch_0_fun/ppermute | solution.py:207
  55.3 15.3 %copy-start.2 = (f32[128]{0:T(128)}, f32[128]{0:T(128)S(1)}, u32[]{:S(2)}) copy-start(f32[128]{0:T(128)S(1)} %get-tuple-element.192) | copy-start | bytes 1540
  89.7 7.5 %collective-permute-start.1 = (f32[16,136,128]{2,1,0:T(8,128)S(1)}, f32[16,136,128]{2,1,0:T(8,128)S(1)}, u32[]{:S(2)}, u32[]{:S(2)}) collective-permute-start(f32[16,136,128]{2,1,0:T(8,128)S(1)} %all_to_all.94.mine), channel_id=1, source_target_pairs={{0,16},{16,0},{1,17},{17,1},{2,18},{18,2},{3,19},{19,3},{4,20},{20... | collective-permute-start | bytes 3342344 | tf_op jit(solution)/shard_map/cond/branch_0_fun/ppermute | solution.py:225
  98.2 1.3 %copy-start.5 = (f32[16,2,128,128]{3,2,1,0:T(8,128)}, f32[16,2,128,128]{3,2,1,0:T(8,128)S(1)}, u32[]{:S(2)}) copy-start(f32[16,2,128,128]{3,2,1,0:T(8,128)S(1)} %get-tuple-element.168) | copy-start | bytes 6291460

commit v6 on v5

--- a/solution.py
+++ b/solution.py
@@ -180,15 +180,16 @@
 
 def column_sums(mean_grad):
     square = mean_grad * mean_grad + 1e-30
-    return jnp.sum(share(jnp.sum(square, 0)[None], DP, Q * C), (0, 1))
+    return share(jnp.sum(square, 0)[None], DP, Q * C)
 
 
 def front(ahead, kept, other, weights):
     if not ahead:
         got = lax.all_to_all(kept + other, "q", 0, 0, tiled=True)
         mean_grad = jnp.sum(got, 0) / (Q * C)
-        none = jnp.zeros((Q, ROWS, COLS), jnp.float32)
-        return mean_grad, column_sums(mean_grad), none, none
+        col_sums = column_sums(mean_grad)
+        none = jnp.broadcast_to(col_sums[:Q], (Q, ROWS, COLS))
+        return mean_grad, col_sums, none, none
 
     def exchange(x, groups):
         return lax.all_to_all(x, DP, 0, 0, axis_index_groups=groups, tiled=True)
@@ -252,6 +253,7 @@
     )
 
     square = mean_grad * mean_grad + 1e-30
+    col_sums = jnp.sum(col_sums, (0, 1))
     col_new = decay_rate * col_state + (1.0 - decay_rate) * (col_sums / D)
     both = jnp.stack(
         [jnp.sum(square, 1), jnp.sum(mean_grad * mean_grad * (1.0 / col_new), 1)]

time: 101 us -> 100 us (0.990)
  no operation moved by 1% of the time
where the time goes in v6:
time: 100 us; the launch traced here: 98.6 us
  blocking collectives  70.6 us (71%)
  starting transfers between devices  18 us (18%)
  waiting for transfers between devices  4.5 us (4%)
  other arithmetic  1.88 us (2%)
  local copies, waits for them, and re-layouts  1.67 us (2%)
  Pallas kernels  1.06 us (1%)
    all_to_all x3, blocking collectives, share(): lax.all_to_all(jnp.broadcast_to(x[None], (n, *x.shape)), axes, 0, 0, tile...  42.9 us
    all_to_all x2, blocking collectives, exchange(): return lax.all_to_all(x, DP, 0, 0, axis_index_groups=groups, tiled=True)  27.8 us
    ppermute x1, starting transfers between devices, per_device(): other = lax.ppermute(sent, 'c', SWAP)  8.79 us
    ppermute x1, starting transfers between devices, back_early(): other = lax.ppermute(mine, 'c', SWAP)  5.18 us
    ppermute x1, starting transfers between devices, front(): others = lax.ppermute(rows, 'c', SWAP)  3.99 us
    ppermute x1, waiting for transfers between devices, back_early(): other = lax.ppermute(mine, 'c', SWAP)  2.36 us
    ppermute x1, waiting for transfers between devices, per_device(): other = lax.ppermute(sent, 'c', SWAP)  2.14 us
  transfers between devices with their start and end apart: 3, of which 2 were waited for; matrix products, arithmetic and copies ran while one was open for 0% of the time, Pallas kernels for 0%

profile of v6, /device:TPU:1, one launch (start us, length us, event | category | flops | bytes accessed | tf_op | source)
XLA Modules:
  0.0 98.6 jit_solution(12499761165552285863)
XLA Ops:
  0.6 0.0 copy-start.1
  0.6 0.0 copy-start
  0.7 1.2 %bitcast_convert_fusion.1 = f32[16,128,128]{2,1,0:T(8,128)S(1)} fusion(bf16[16,2,128,128]{3,2,1,0:T(8,128)(2,1)} %bitcast.48, s32[]{:T(128)S(6)} %select_n.7), kind=kLoop, calls=%fused_computation.27 | loop fusion | flops 262144 | bytes 1572868 | tf_op jit(solution)/shard_map/convert_element_type | solution.py:245
  1.9 8.8 %collective-permute-start.9 = (f32[16,128,128]{2,1,0:T(8,128)S(1)}, f32[16,128,128]{2,1,0:T(8,128)S(1)}, u32[]{:S(2)}, u32[]{:S(2)}) collective-permute-start(f32[16,128,128]{2,1,0:T(8,128)S(1)} %bitcast_convert_fusion.1), channel_id=1, source_target_pairs={{0,16},{16,0},{1,17},{17,1},{2,18},{18,2},{3,19},{19,3},{4,20},{20... | collective-permute-start | bytes 3145736 | tf_op jit(solution)/shard_map/ppermute | solution.py:247
  10.7 0.0 copy-done.1
  10.7 0.1 bitcast_convert_fusion
  10.8 2.1 %collective-permute-done.9 = f32[16,128,128]{2,1,0:T(8,128)S(1)} collective-permute-done((f32[16,128,128]{2,1,0:T(8,128)S(1)}, f32[16,128,128]{2,1,0:T(8,128)S(1)}, u32[]{:S(2)}, u32[]{:S(2)}) %collective-permute-start.9) | collective-permute-done | bytes 1048608 | tf_op jit(solution)/shard_map/ppermute | solution.py:247
  13.0 0.0 copy-done
  13.0 0.0 copy-start.4
  13.0 0.0 copy-start.3
  13.0 42.4 %conditional.2 = (f32[128,128]{1,0:T(8,128)S(1)}, f32[16,128,128]{2,1,0:T(8,128)S(1)}, f32[16,128,128]{2,1,0:T(8,128)S(1)}, f32[128,128]{1,0:T(8,128)S(1)}, f32[128]{0:T(128)S(1)}) conditional(s32[]{:T(128)} %clamp.4, (f32[16,128,128]{2,1,0:T(8,128)S(1)}, f32[16,128,128]{2,1,0:T(8,128)S(1)}, ...), branch_computations={%region_0.5_spmd, %region_5.10_spmd, %region_10.15_spmd, %region_1... | conditional | flops 642816 | bytes 17892948 | solution.py:251
  13.0 0.1 arrange.4
  13.1 13.9 %all_to_all.85 = f32[4,640,128]{2,1,0:T(8,128)S(1)} all-to-all(f32[4,640,128]{2,1,0:T(8,128)S(1)} %arrange.4), channel_id=1, replica_groups={{0,32,64,96},{128,160,192,224},{256,288,320,352},{384,416,448,480},{16,..., dimensions={0} | all-to-all | bytes 2621440 | tf_op jit(solution)/shard_map/cond/branch_0_fun/all_to_all | solution.py:195
  27.0 0.1 slice_reduce_fusion
  27.0 0.1 broadcast_in_dim.43
  27.1 0.1 pad_maximum_fusion
  27.2 13.9 %all_to_all.86 = f32[4,640,128]{2,1,0:T(8,128)S(1)} all-to-all(f32[4,640,128]{2,1,0:T(8,128)S(1)} %pad_maximum_fusion), channel_id=1, replica_groups={{0,128,256,384},{32,160,288,416},{64,192,320,448},{96,224,352,480},{16,..., dimensions={0} | all-to-all | bytes 2621440 | tf_op jit(solution)/shard_map/cond/branch_0_fun/all_to_all | solution.py:195
  41.1 0.1 slice.80
  41.2 4.0 %collective-permute-start.8 = (f32[16,128,128]{2,1,0:T(8,128)S(1)}, f32[16,128,128]{2,1,0:T(8,128)S(1)}, u32[]{:S(2)}, u32[]{:S(2)}) collective-permute-start(f32[16,128,128]{2,1,0:T(8,128)S(1)} %bitcast.39), channel_id=1, source_target_pairs={{0,16},{16,0},{1,17},{17,1},{2,18},{18,2},{3,19},{19,3},{4,20},{20... | collective-permute-start | bytes 3145736 | tf_op jit(solution)/shard_map/cond/branch_0_fun/ppermute | solution.py:208
  45.2 10.1 %all_to_all.87 = f32[32,1,128]{2,1,0:T(1,128)S(1)} all-to-all(f32[32,1,128]{2,1,0:T(1,128)S(1)} %broadcast_in_dim.44), channel_id=1, replica_groups=mesh['q'=16,'c'=2,'z'=16] {'q','c'}, dimensions={0} | all-to-all | bytes 32768 | tf_op jit(solution)/shard_map/cond/branch_0_fun/all_to_all | solution.py:30
  55.3 0.0 collective-permute-done.8
  55.3 0.0 copy-done.4
  55.3 0.0 copy-start.2
  55.4 0.1 add_reduce_fusion.5
  55.5 14.0 %all_to_all.102 = f32[16,2,128]{2,1,0:T(2,128)S(1)} all-to-all(f32[16,2,128]{2,1,0:T(2,128)S(1)} %broadcast_in_dim.77), channel_id=1, replica_groups=mesh['q'=16,'c'=2,'z'=16] {'z'}, dimensions={0} | all-to-all | bytes 32768 | tf_op jit(solution)/shard_map/all_to_all | solution.py:30
  69.6 0.0 copy-done.3
  69.6 0.1 rsqrt_multiply_fusion
  69.7 0.0 copy-done.2
  69.7 27.6 %conditional.3 = (f32[128,128]{1,0:T(8,128)}, f32[16,2,128,128]{3,2,1,0:T(8,128)S(1)}, f32[1,1]{1,0:T(1,128)}, f32[1,128]{1,0:T(1,128)}) conditional(s32[]{:T(128)} %clamp.4, (f32[128,128]{1,0:T(8,128)S(1)}, f32[2,128]{1,0:T(2,128)S(1)}, f32[16,128,128]{2,1,0:T(8,128)S(1)}, f32[16,128,128]{2,1,0:T(8,128)S(1)}, ...), branch_computations={%region_27.28_spmd, %region_28.29_spmd, %region_29.30_spmd, %regio... | conditional | flops 79872 | bytes 15072040 | solution.py:265
  69.7 0.1 pad.22.clone
  69.8 0.1 maximum_maximum_fusion
  69.9 0.1 broadcast_in_dim.71
  70.0 18.8 %all_to_all.96.mine = f32[16,136,128]{2,1,0:T(8,128)S(1)} all-to-all(f32[16,136,128]{2,1,0:T(8,128)S(1)} %broadcast_in_dim.71), channel_id=1, replica_groups=mesh['q'=16,'c'=2,'z'=16] {'q'}, dimensions={0} | all-to-all | bytes 2228224 | tf_op jit(solution)/shard_map/cond/branch_0_fun/all_to_all | solution.py:30
  88.8 5.2 %collective-permute-start.1 = (f32[16,136,128]{2,1,0:T(8,128)S(1)}, f32[16,136,128]{2,1,0:T(8,128)S(1)}, u32[]{:S(2)}, u32[]{:S(2)}) collective-permute-start(f32[16,136,128]{2,1,0:T(8,128)S(1)} %all_to_all.96.mine), channel_id=1, source_target_pairs={{0,16},{16,0},{1,17},{17,1},{2,18},{18,2},{3,19},{19,3},{4,20},{20... | collective-permute-start | bytes 3342344 | tf_op jit(solution)/shard_map/cond/branch_0_fun/ppermute | solution.py:226
  94.0 2.4 %collective-permute-done.1.other = f32[16,136,128]{2,1,0:T(8,128)S(1)} collective-permute-done((f32[16,136,128]{2,1,0:T(8,128)S(1)}, f32[16,136,128]{2,1,0:T(8,128)S(1)}, u32[]{:S(2)}, u32[]{:S(2)}) %collective-permute-start.1) | collective-permute-done | bytes 1114144 | tf_op jit(solution)/shard_map/cond/branch_0_fun/ppermute | solution.py:226
  96.3 0.9 finish.4
  97.3 0.0 copy-start.5
  97.3 1.3 %copy-done.5 = f32[16,2,128,128]{3,2,1,0:T(8,128)} copy-done((f32[16,2,128,128]{3,2,1,0:T(8,128)}, f32[16,2,128,128]{3,2,1,0:T(8,128)S(1)}, u32[]{:S(2)}) %copy-start.5) | copy-done | bytes 2097176
  (12 shorter events, 0.2 us)
Async XLA Ops:
  0.6 10.1 %copy-start.1 = (bf16[1,4096,128]{2,1,0:T(8,128)(2,1)S(1)}, bf16[1,4096,128]{2,1,0:T(8,128)(2,1)}, u32[]{:S(2)}) copy-start(bf16[1,4096,128]{2,1,0:T(8,128)(2,1)} %param.14) | copy-start | bytes 3145732
  0.6 12.3 %copy-start = (f32[128,128]{1,0:T(8,128)S(1)}, f32[128,128]{1,0:T(8,128)}, u32[]{:S(2)}) copy-start(f32[128,128]{1,0:T(8,128)} %param.15) | copy-start | bytes 196612
  1.9 11.1 %collective-permute-start.9 = (f32[16,128,128]{2,1,0:T(8,128)S(1)}, f32[16,128,128]{2,1,0:T(8,128)S(1)}, u32[]{:S(2)}, u32[]{:S(2)}) collective-permute-start(f32[16,128,128]{2,1,0:T(8,128)S(1)} %bitcast_convert_fusion.1), channel_id=1, source_target_pairs={{0,16},{16,0},{1,17},{17,1},{2,18},{18,2},{3,19},{19,3},{4,20},{20... | collective-permute-start | bytes 3145736 | tf_op jit(solution)/shard_map/ppermute | solution.py:247
  13.0 42.4 %copy-start.4 = (f32[128]{0:T(128)S(1)}, f32[128]{0:T(128)}, u32[]{:S(2)}) copy-start(f32[128]{0:T(128)} %param.17) | copy-start | bytes 1540
  13.0 56.6 %copy-start.3 = (f32[128]{0:T(128)S(1)}, f32[128]{0:T(128)}, u32[]{:S(2)}) copy-start(f32[128]{0:T(128)} %param.16) | copy-start | bytes 1540
  41.2 14.2 %collective-permute-start.8 = (f32[16,128,128]{2,1,0:T(8,128)S(1)}, f32[16,128,128]{2,1,0:T(8,128)S(1)}, u32[]{:S(2)}, u32[]{:S(2)}) collective-permute-start(f32[16,128,128]{2,1,0:T(8,128)S(1)} %bitcast.39), channel_id=1, source_target_pairs={{0,16},{16,0},{1,17},{17,1},{2,18},{18,2},{3,19},{19,3},{4,20},{20... | collective-permute-start | bytes 3145736 | tf_op jit(solution)/shard_map/cond/branch_0_fun/ppermute | solution.py:208
  55.3 14.3 %copy-start.2 = (f32[128]{0:T(128)}, f32[128]{0:T(128)S(1)}, u32[]{:S(2)}) copy-start(f32[128]{0:T(128)S(1)} %get-tuple-element.193) | copy-start | bytes 1540
  88.8 7.5 %collective-permute-start.1 = (f32[16,136,128]{2,1,0:T(8,128)S(1)}, f32[16,136,128]{2,1,0:T(8,128)S(1)}, u32[]{:S(2)}, u32[]{:S(2)}) collective-permute-start(f32[16,136,128]{2,1,0:T(8,128)S(1)} %all_to_all.96.mine), channel_id=1, source_target_pairs={{0,16},{16,0},{1,17},{17,1},{2,18},{18,2},{3,19},{19,3},{4,20},{20... | collective-permute-start | bytes 3342344 | tf_op jit(solution)/shard_map/cond/branch_0_fun/ppermute | solution.py:226
  97.3 1.3 %copy-start.5 = (f32[16,2,128,128]{3,2,1,0:T(8,128)}, f32[16,2,128,128]{3,2,1,0:T(8,128)S(1)}, u32[]{:S(2)}) copy-start(f32[16,2,128,128]{3,2,1,0:T(8,128)S(1)} %get-tuple-element.169) | copy-start | bytes 6291460

commit v7 on v6

--- a/solution.py
+++ b/solution.py
@@ -13,7 +13,7 @@
 Q, C, Z = 16, 2, 16
 ROWS = D // (Q * C)
 COLS = FLAT // Z
-AHEAD = (128, 112, 80, 56, 0)
+AHEAD = (128, 112, 64, 40, 0)
 SIDE = range(4)
 ALONG_X = [[[(y * 4 + x) * C + c for x in SIDE] for y in SIDE] for c in range(C)]
 ALONG_Y = [[[(y * 4 + x) * C + c for y in SIDE] for x in SIDE] for c in range(C)]
@@ -247,7 +247,8 @@
     other = lax.ppermute(sent, "c", SWAP)
     kept = lax.dynamic_index_in_dim(grads, core, 1, False)
     kept = lax.optimization_barrier(kept.astype(jnp.float32))
-    plane = jnp.clip(lax.axis_index("z") - 2, 0, len(AHEAD) - 1)
+    z = lax.axis_index("z")
+    plane = jnp.where(z < 4, z // 2, jnp.minimum(z - 2, len(AHEAD) - 1))
     mean_grad, col_sums, own, others = lax.switch(
         plane, [functools.partial(front, n) for n in AHEAD], kept, other, weights
     )

time: 100 us -> 101 us (1.010)
  no operation moved by 1% of the time
where the time goes in v7:
time: 101 us; the launch traced here: 99.4 us
  blocking collectives  70.4 us (70%)
  starting transfers between devices  17.8 us (18%)
  waiting for transfers between devices  4.7 us (5%)
  other arithmetic  2.87 us (3%)
  local copies, waits for them, and re-layouts  1.67 us (2%)
  Pallas kernels  1.06 us (1%)
    all_to_all x3, blocking collectives, share(): lax.all_to_all(jnp.broadcast_to(x[None], (n, *x.shape)), axes, 0, 0, tile...  42.7 us
    all_to_all x2, blocking collectives, exchange(): return lax.all_to_all(x, DP, 0, 0, axis_index_groups=groups, tiled=True)  27.8 us
    ppermute x1, starting transfers between devices, per_device(): other = lax.ppermute(sent, 'c', SWAP)  8.77 us
    ppermute x1, starting transfers between devices, back_early(): other = lax.ppermute(mine, 'c', SWAP)  4.99 us
    ppermute x1, starting transfers between devices, front(): others = lax.ppermute(rows, 'c', SWAP)  3.99 us
    ppermute x1, waiting for transfers between devices, back_early(): other = lax.ppermute(mine, 'c', SWAP)  2.36 us
    ppermute x1, waiting for transfers between devices, per_device(): other = lax.ppermute(sent, 'c', SWAP)  2.34 us
    convert_element_type x1, other arithmetic, per_device(): lax.dynamic_index_in_dim(grads, 1 - core, 1, False).astype(jnp.float32)  2.21 us
  transfers between devices with their start and end apart: 3, of which 2 were waited for; matrix products, arithmetic and copies ran while one was open for 0% of the time, Pallas kernels for 0%

profile of v7, /device:TPU:1, one launch (start us, length us, event | category | flops | bytes accessed | tf_op | source)
XLA Modules:
  0.0 99.4 jit_solution(8588441573248602081)
XLA Ops:
  0.6 0.0 copy-start.1
  0.6 0.0 copy-start
  0.7 2.2 %bitcast_convert_fusion.1 = f32[16,128,128]{2,1,0:T(8,128)} fusion(bf16[16,2,128,128]{3,2,1,0:T(8,128)(2,1)} %bitcast.47, s32[]{:T(128)S(6)} %select_n.17), kind=kLoop, calls=%fused_computation.27 | loop fusion | flops 262144 | bytes 1572868 | tf_op jit(solution)/shard_map/convert_element_type | solution.py:245
  2.9 8.8 %collective-permute-start.9 = (f32[16,128,128]{2,1,0:T(8,128)}, f32[16,128,128]{2,1,0:T(8,128)S(1)}, u32[]{:S(2)}, u32[]{:S(2)}) collective-permute-start(f32[16,128,128]{2,1,0:T(8,128)} %bitcast_convert_fusion.1), channel_id=1, source_target_pairs={{0,16},{16,0},{1,17},{17,1},{2,18},{18,2},{3,19},{19,3},{4,20},{20... | collective-permute-start | bytes 3145736 | tf_op jit(solution)/shard_map/ppermute | solution.py:247
  11.7 0.0 copy-done.1
  11.7 0.1 bitcast_convert_fusion
  11.8 2.3 %collective-permute-done.9 = f32[16,128,128]{2,1,0:T(8,128)S(1)} collective-permute-done((f32[16,128,128]{2,1,0:T(8,128)}, f32[16,128,128]{2,1,0:T(8,128)S(1)}, u32[]{:S(2)}, u32[]{:S(2)}) %collective-permute-start.9) | collective-permute-done | bytes 1048608 | tf_op jit(solution)/shard_map/ppermute | solution.py:247
  14.1 0.0 copy-done
  14.1 0.0 copy-start.4
  14.1 0.0 copy-start.3
  14.1 42.4 %conditional.2 = (f32[128,128]{1,0:T(8,128)S(1)}, f32[16,128,128]{2,1,0:T(8,128)S(1)}, f32[16,128,128]{2,1,0:T(8,128)S(1)}, f32[128,128]{1,0:T(8,128)S(1)}, f32[128]{0:T(128)S(1)}) conditional(s32[]{:T(128)} %clamp.4, (f32[16,128,128]{2,1,0:T(8,128)S(1)}, f32[16,128,128]{2,1,0:T(8,128)S(1)}, ...), branch_computations={%region_0.5_spmd, %region_5.10_spmd, %region_10.15_spmd, %region_1... | conditional | flops 642816 | bytes 17892948 | solution.py:252
  14.1 0.1 arrange.4
  14.3 13.9 %all_to_all.85 = f32[4,640,128]{2,1,0:T(8,128)S(1)} all-to-all(f32[4,640,128]{2,1,0:T(8,128)S(1)} %arrange.4), channel_id=1, replica_groups={{0,32,64,96},{128,160,192,224},{256,288,320,352},{384,416,448,480},{16,..., dimensions={0} | all-to-all | bytes 2621440 | tf_op jit(solution)/shard_map/cond/branch_0_fun/all_to_all | solution.py:195
  28.2 0.1 slice_reduce_fusion
  28.2 0.1 broadcast_in_dim.43
  28.3 0.1 pad_maximum_fusion
  28.4 13.9 %all_to_all.86 = f32[4,640,128]{2,1,0:T(8,128)S(1)} all-to-all(f32[4,640,128]{2,1,0:T(8,128)S(1)} %pad_maximum_fusion), channel_id=1, replica_groups={{0,128,256,384},{32,160,288,416},{64,192,320,448},{96,224,352,480},{16,..., dimensions={0} | all-to-all | bytes 2621440 | tf_op jit(solution)/shard_map/cond/branch_0_fun/all_to_all | solution.py:195
  42.3 0.1 slice.80
  42.3 4.0 %collective-permute-start.8 = (f32[16,128,128]{2,1,0:T(8,128)S(1)}, f32[16,128,128]{2,1,0:T(8,128)S(1)}, u32[]{:S(2)}, u32[]{:S(2)}) collective-permute-start(f32[16,128,128]{2,1,0:T(8,128)S(1)} %bitcast.39), channel_id=1, source_target_pairs={{0,16},{16,0},{1,17},{17,1},{2,18},{18,2},{3,19},{19,3},{4,20},{20... | collective-permute-start | bytes 3145736 | tf_op jit(solution)/shard_map/cond/branch_0_fun/ppermute | solution.py:208
  46.4 10.1 %all_to_all.87 = f32[32,1,128]{2,1,0:T(1,128)S(1)} all-to-all(f32[32,1,128]{2,1,0:T(1,128)S(1)} %broadcast_in_dim.44), channel_id=1, replica_groups=mesh['q'=16,'c'=2,'z'=16] {'q','c'}, dimensions={0} | all-to-all | bytes 32768 | tf_op jit(solution)/shard_map/cond/branch_0_fun/all_to_all | solution.py:30
  56.5 0.0 collective-permute-done.8
  56.5 0.0 copy-done.4
  56.5 0.0 copy-start.2
  56.5 0.1 add_reduce_fusion.5
  56.7 13.8 %all_to_all.102 = f32[16,2,128]{2,1,0:T(2,128)S(1)} all-to-all(f32[16,2,128]{2,1,0:T(2,128)S(1)} %broadcast_in_dim.77), channel_id=1, replica_groups=mesh['q'=16,'c'=2,'z'=16] {'z'}, dimensions={0} | all-to-all | bytes 32768 | tf_op jit(solution)/shard_map/all_to_all | solution.py:30
  70.5 0.0 copy-done.3
  70.5 0.1 rsqrt_multiply_fusion
  70.7 0.0 copy-done.2
  70.7 27.4 %conditional.3 = (f32[128,128]{1,0:T(8,128)}, f32[16,2,128,128]{3,2,1,0:T(8,128)S(1)}, f32[1,1]{1,0:T(1,128)}, f32[1,128]{1,0:T(1,128)}) conditional(s32[]{:T(128)} %clamp.4, (f32[128,128]{1,0:T(8,128)S(1)}, f32[2,128]{1,0:T(2,128)S(1)}, f32[16,128,128]{2,1,0:T(8,128)S(1)}, f32[16,128,128]{2,1,0:T(8,128)S(1)}, ...), branch_computations={%region_27.28_spmd, %region_28.29_spmd, %region_29.30_spmd, %regio... | conditional | flops 86016 | bytes 15244200 | solution.py:266
  70.7 0.1 pad.22.clone
  70.8 0.1 maximum_maximum_fusion
  70.9 0.1 broadcast_in_dim.71
  70.9 18.8 %all_to_all.96.mine = f32[16,136,128]{2,1,0:T(8,128)S(1)} all-to-all(f32[16,136,128]{2,1,0:T(8,128)S(1)} %broadcast_in_dim.71), channel_id=1, replica_groups=mesh['q'=16,'c'=2,'z'=16] {'q'}, dimensions={0} | all-to-all | bytes 2228224 | tf_op jit(solution)/shard_map/cond/branch_0_fun/all_to_all | solution.py:30
  89.8 5.0 %collective-permute-start.1 = (f32[16,136,128]{2,1,0:T(8,128)S(1)}, f32[16,136,128]{2,1,0:T(8,128)S(1)}, u32[]{:S(2)}, u32[]{:S(2)}) collective-permute-start(f32[16,136,128]{2,1,0:T(8,128)S(1)} %all_to_all.96.mine), channel_id=1, source_target_pairs={{0,16},{16,0},{1,17},{17,1},{2,18},{18,2},{3,19},{19,3},{4,20},{20... | collective-permute-start | bytes 3342344 | tf_op jit(solution)/shard_map/cond/branch_0_fun/ppermute | solution.py:226
  94.8 2.4 %collective-permute-done.1.other = f32[16,136,128]{2,1,0:T(8,128)S(1)} collective-permute-done((f32[16,136,128]{2,1,0:T(8,128)S(1)}, f32[16,136,128]{2,1,0:T(8,128)S(1)}, u32[]{:S(2)}, u32[]{:S(2)}) %collective-permute-start.1) | collective-permute-done | bytes 1114144 | tf_op jit(solution)/shard_map/cond/branch_0_fun/ppermute | solution.py:226
  97.1 0.9 finish.4
  98.1 0.0 copy-start.5
  98.1 1.3 %copy-done.5 = f32[16,2,128,128]{3,2,1,0:T(8,128)} copy-done((f32[16,2,128,128]{3,2,1,0:T(8,128)}, f32[16,2,128,128]{3,2,1,0:T(8,128)S(1)}, u32[]{:S(2)}) %copy-start.5) | copy-done | bytes 2097176
  (12 shorter events, 0.2 us)
Async XLA Ops:
  0.6 11.0 %copy-start.1 = (bf16[1,4096,128]{2,1,0:T(8,128)(2,1)S(1)}, bf16[1,4096,128]{2,1,0:T(8,128)(2,1)}, u32[]{:S(2)}) copy-start(bf16[1,4096,128]{2,1,0:T(8,128)(2,1)} %param.14) | copy-start | bytes 3145732
  0.6 13.5 %copy-start = (f32[128,128]{1,0:T(8,128)S(1)}, f32[128,128]{1,0:T(8,128)}, u32[]{:S(2)}) copy-start(f32[128,128]{1,0:T(8,128)} %param.15) | copy-start | bytes 196612
  2.9 11.3 %collective-permute-start.9 = (f32[16,128,128]{2,1,0:T(8,128)}, f32[16,128,128]{2,1,0:T(8,128)S(1)}, u32[]{:S(2)}, u32[]{:S(2)}) collective-permute-start(f32[16,128,128]{2,1,0:T(8,128)} %bitcast_convert_fusion.1), channel_id=1, source_target_pairs={{0,16},{16,0},{1,17},{17,1},{2,18},{18,2},{3,19},{19,3},{4,20},{20... | collective-permute-start | bytes 3145736 | tf_op jit(solution)/shard_map/ppermute | solution.py:247
  14.1 42.4 %copy-start.4 = (f32[128]{0:T(128)S(1)}, f32[128]{0:T(128)}, u32[]{:S(2)}) copy-start(f32[128]{0:T(128)} %param.17) | copy-start | bytes 1540
  14.1 56.4 %copy-start.3 = (f32[128]{0:T(128)S(1)}, f32[128]{0:T(128)}, u32[]{:S(2)}) copy-start(f32[128]{0:T(128)} %param.16) | copy-start | bytes 1540
  42.3 14.2 %collective-permute-start.8 = (f32[16,128,128]{2,1,0:T(8,128)S(1)}, f32[16,128,128]{2,1,0:T(8,128)S(1)}, u32[]{:S(2)}, u32[]{:S(2)}) collective-permute-start(f32[16,128,128]{2,1,0:T(8,128)S(1)} %bitcast.39), channel_id=1, source_target_pairs={{0,16},{16,0},{1,17},{17,1},{2,18},{18,2},{3,19},{19,3},{4,20},{20... | collective-permute-start | bytes 3145736 | tf_op jit(solution)/shard_map/cond/branch_0_fun/ppermute | solution.py:208
  56.5 14.1 %copy-start.2 = (f32[128]{0:T(128)}, f32[128]{0:T(128)S(1)}, u32[]{:S(2)}) copy-start(f32[128]{0:T(128)S(1)} %get-tuple-element.193) | copy-start | bytes 1540
  89.8 7.4 %collective-permute-start.1 = (f32[16,136,128]{2,1,0:T(8,128)S(1)}, f32[16,136,128]{2,1,0:T(8,128)S(1)}, u32[]{:S(2)}, u32[]{:S(2)}) collective-permute-start(f32[16,136,128]{2,1,0:T(8,128)S(1)} %all_to_all.96.mine), channel_id=1, source_target_pairs={{0,16},{16,0},{1,17},{17,1},{2,18},{18,2},{3,19},{19,3},{4,20},{20... | collective-permute-start | bytes 3342344 | tf_op jit(solution)/shard_map/cond/branch_0_fun/ppermute | solution.py:226
  98.1 1.3 %copy-start.5 = (f32[16,2,128,128]{3,2,1,0:T(8,128)}, f32[16,2,128,128]{3,2,1,0:T(8,128)S(1)}, u32[]{:S(2)}) copy-start(f32[16,2,128,128]{3,2,1,0:T(8,128)S(1)} %get-tuple-element.169) | copy-start | bytes 6291460

commit v8 on v7

--- a/solution.py
+++ b/solution.py
@@ -13,7 +13,7 @@
 Q, C, Z = 16, 2, 16
 ROWS = D // (Q * C)
 COLS = FLAT // Z
-AHEAD = (128, 112, 64, 40, 0)
+AHEAD = (128, 112, 72, 48, 0)
 SIDE = range(4)
 ALONG_X = [[[(y * 4 + x) * C + c for x in SIDE] for y in SIDE] for c in range(C)]
 ALONG_Y = [[[(y * 4 + x) * C + c for y in SIDE] for x in SIDE] for c in range(C)]

time: 101 us -> 101 us (level)
  no operation moved by 1% of the time
where the time goes in v8:
time: 101 us; the launch traced here: 99.4 us
  blocking collectives  70.4 us (70%)
  starting transfers between devices  17.8 us (18%)
  waiting for transfers between devices  4.7 us (5%)
  other arithmetic  2.87 us (3%)
  local copies, waits for them, and re-layouts  1.67 us (2%)
  Pallas kernels  1.06 us (1%)
    all_to_all x3, blocking collectives, share(): lax.all_to_all(jnp.broadcast_to(x[None], (n, *x.shape)), axes, 0, 0, tile...  42.7 us
    all_to_all x2, blocking collectives, exchange(): return lax.all_to_all(x, DP, 0, 0, axis_index_groups=groups, tiled=True)  27.8 us
    ppermute x1, starting transfers between devices, per_device(): other = lax.ppermute(sent, 'c', SWAP)  8.77 us
    ppermute x1, starting transfers between devices, back_early(): other = lax.ppermute(mine, 'c', SWAP)  4.99 us
    ppermute x1, starting transfers between devices, front(): others = lax.ppermute(rows, 'c', SWAP)  3.99 us
    ppermute x1, waiting for transfers between devices, back_early(): other = lax.ppermute(mine, 'c', SWAP)  2.36 us
    ppermute x1, waiting for transfers between devices, per_device(): other = lax.ppermute(sent, 'c', SWAP)  2.34 us
    convert_element_type x1, other arithmetic, per_device(): lax.dynamic_index_in_dim(grads, 1 - core, 1, False).astype(jnp.float32)  2.21 us
  transfers between devices with their start and end apart: 3, of which 2 were waited for; matrix products, arithmetic and copies ran while one was open for 0% of the time, Pallas kernels for 0%

profile of v8, /device:TPU:1, one launch (start us, length us, event | category | flops | bytes accessed | tf_op | source)
XLA Modules:
  0.0 99.4 jit_solution(12133054101039062527)
XLA Ops:
  0.6 0.0 copy-start.1
  0.6 0.0 copy-start
  0.7 2.2 %bitcast_convert_fusion.1 = f32[16,128,128]{2,1,0:T(8,128)} fusion(bf16[16,2,128,128]{3,2,1,0:T(8,128)(2,1)} %bitcast.48, s32[]{:T(128)S(6)} %select_n.17), kind=kLoop, calls=%fused_computation.27 | loop fusion | flops 262144 | bytes 1572868 | tf_op jit(solution)/shard_map/convert_element_type | solution.py:245
  2.9 8.8 %collective-permute-start.9 = (f32[16,128,128]{2,1,0:T(8,128)}, f32[16,128,128]{2,1,0:T(8,128)S(1)}, u32[]{:S(2)}, u32[]{:S(2)}) collective-permute-start(f32[16,128,128]{2,1,0:T(8,128)} %bitcast_convert_fusion.1), channel_id=1, source_target_pairs={{0,16},{16,0},{1,17},{17,1},{2,18},{18,2},{3,19},{19,3},{4,20},{20... | collective-permute-start | bytes 3145736 | tf_op jit(solution)/shard_map/ppermute | solution.py:247
  11.7 0.0 copy-done.1
  11.7 0.1 bitcast_convert_fusion
  11.8 2.3 %collective-permute-done.9 = f32[16,128,128]{2,1,0:T(8,128)S(1)} collective-permute-done((f32[16,128,128]{2,1,0:T(8,128)}, f32[16,128,128]{2,1,0:T(8,128)S(1)}, u32[]{:S(2)}, u32[]{:S(2)}) %collective-permute-start.9) | collective-permute-done | bytes 1048608 | tf_op jit(solution)/shard_map/ppermute | solution.py:247
  14.1 0.0 copy-done
  14.1 0.0 copy-start.4
  14.1 0.0 copy-start.3
  14.1 42.4 %conditional.2 = (f32[128,128]{1,0:T(8,128)S(1)}, f32[16,128,128]{2,1,0:T(8,128)S(1)}, f32[16,128,128]{2,1,0:T(8,128)S(1)}, f32[128,128]{1,0:T(8,128)S(1)}, f32[128]{0:T(128)S(1)}) conditional(s32[]{:T(128)} %clamp.4, (f32[16,128,128]{2,1,0:T(8,128)S(1)}, f32[16,128,128]{2,1,0:T(8,128)S(1)}, ...), branch_computations={%region_0.5_spmd, %region_5.10_spmd, %region_10.15_spmd, %region_1... | conditional | flops 642816 | bytes 17892948 | solution.py:252
  14.1 0.1 arrange.4
  14.3 13.9 %all_to_all.85 = f32[4,640,128]{2,1,0:T(8,128)S(1)} all-to-all(f32[4,640,128]{2,1,0:T(8,128)S(1)} %arrange.4), channel_id=1, replica_groups={{0,32,64,96},{128,160,192,224},{256,288,320,352},{384,416,448,480},{16,..., dimensions={0} | all-to-all | bytes 2621440 | tf_op jit(solution)/shard_map/cond/branch_0_fun/all_to_all | solution.py:195
  28.2 0.1 slice_reduce_fusion
  28.2 0.1 broadcast_in_dim.43
  28.3 0.1 pad_maximum_fusion
  28.4 13.9 %all_to_all.86 = f32[4,640,128]{2,1,0:T(8,128)S(1)} all-to-all(f32[4,640,128]{2,1,0:T(8,128)S(1)} %pad_maximum_fusion), channel_id=1, replica_groups={{0,128,256,384},{32,160,288,416},{64,192,320,448},{96,224,352,480},{16,..., dimensions={0} | all-to-all | bytes 2621440 | tf_op jit(solution)/shard_map/cond/branch_0_fun/all_to_all | solution.py:195
  42.3 0.1 slice.80
  42.3 4.0 %collective-permute-start.8 = (f32[16,128,128]{2,1,0:T(8,128)S(1)}, f32[16,128,128]{2,1,0:T(8,128)S(1)}, u32[]{:S(2)}, u32[]{:S(2)}) collective-permute-start(f32[16,128,128]{2,1,0:T(8,128)S(1)} %bitcast.39), channel_id=1, source_target_pairs={{0,16},{16,0},{1,17},{17,1},{2,18},{18,2},{3,19},{19,3},{4,20},{20... | collective-permute-start | bytes 3145736 | tf_op jit(solution)/shard_map/cond/branch_0_fun/ppermute | solution.py:208
  46.4 10.1 %all_to_all.87 = f32[32,1,128]{2,1,0:T(1,128)S(1)} all-to-all(f32[32,1,128]{2,1,0:T(1,128)S(1)} %broadcast_in_dim.44), channel_id=1, replica_groups=mesh['q'=16,'c'=2,'z'=16] {'q','c'}, dimensions={0} | all-to-all | bytes 32768 | tf_op jit(solution)/shard_map/cond/branch_0_fun/all_to_all | solution.py:30
  56.5 0.0 collective-permute-done.8
  56.5 0.0 copy-done.4
  56.5 0.0 copy-start.2
  56.5 0.1 add_reduce_fusion.5
  56.7 13.8 %all_to_all.102 = f32[16,2,128]{2,1,0:T(2,128)S(1)} all-to-all(f32[16,2,128]{2,1,0:T(2,128)S(1)} %broadcast_in_dim.77), channel_id=1, replica_groups=mesh['q'=16,'c'=2,'z'=16] {'z'}, dimensions={0} | all-to-all | bytes 32768 | tf_op jit(solution)/shard_map/all_to_all | solution.py:30
  70.5 0.0 copy-done.3
  70.5 0.1 rsqrt_multiply_fusion
  70.7 0.0 copy-done.2
  70.7 27.4 %conditional.3 = (f32[128,128]{1,0:T(8,128)}, f32[16,2,128,128]{3,2,1,0:T(8,128)S(1)}, f32[1,1]{1,0:T(1,128)}, f32[1,128]{1,0:T(1,128)}) conditional(s32[]{:T(128)} %clamp.4, (f32[128,128]{1,0:T(8,128)S(1)}, f32[2,128]{1,0:T(2,128)S(1)}, f32[16,128,128]{2,1,0:T(8,128)S(1)}, f32[16,128,128]{2,1,0:T(8,128)S(1)}, ...), branch_computations={%region_27.28_spmd, %region_28.29_spmd, %region_29.30_spmd, %regio... | conditional | flops 82944 | bytes 15158120 | solution.py:266
  70.7 0.1 pad.22.clone
  70.8 0.1 maximum_maximum_fusion
  70.9 0.1 broadcast_in_dim.71
  70.9 18.8 %all_to_all.96.mine = f32[16,136,128]{2,1,0:T(8,128)S(1)} all-to-all(f32[16,136,128]{2,1,0:T(8,128)S(1)} %broadcast_in_dim.71), channel_id=1, replica_groups=mesh['q'=16,'c'=2,'z'=16] {'q'}, dimensions={0} | all-to-all | bytes 2228224 | tf_op jit(solution)/shard_map/cond/branch_0_fun/all_to_all | solution.py:30
  89.8 5.0 %collective-permute-start.1 = (f32[16,136,128]{2,1,0:T(8,128)S(1)}, f32[16,136,128]{2,1,0:T(8,128)S(1)}, u32[]{:S(2)}, u32[]{:S(2)}) collective-permute-start(f32[16,136,128]{2,1,0:T(8,128)S(1)} %all_to_all.96.mine), channel_id=1, source_target_pairs={{0,16},{16,0},{1,17},{17,1},{2,18},{18,2},{3,19},{19,3},{4,20},{20... | collective-permute-start | bytes 3342344 | tf_op jit(solution)/shard_map/cond/branch_0_fun/ppermute | solution.py:226
  94.8 2.4 %collective-permute-done.1.other = f32[16,136,128]{2,1,0:T(8,128)S(1)} collective-permute-done((f32[16,136,128]{2,1,0:T(8,128)S(1)}, f32[16,136,128]{2,1,0:T(8,128)S(1)}, u32[]{:S(2)}, u32[]{:S(2)}) %collective-permute-start.1) | collective-permute-done | bytes 1114144 | tf_op jit(solution)/shard_map/cond/branch_0_fun/ppermute | solution.py:226
  97.1 0.9 finish.4
  98.1 0.0 copy-start.5
  98.1 1.3 %copy-done.5 = f32[16,2,128,128]{3,2,1,0:T(8,128)} copy-done((f32[16,2,128,128]{3,2,1,0:T(8,128)}, f32[16,2,128,128]{3,2,1,0:T(8,128)S(1)}, u32[]{:S(2)}) %copy-start.5) | copy-done | bytes 2097176
  (12 shorter events, 0.2 us)
Async XLA Ops:
  0.6 11.0 %copy-start.1 = (bf16[1,4096,128]{2,1,0:T(8,128)(2,1)S(1)}, bf16[1,4096,128]{2,1,0:T(8,128)(2,1)}, u32[]{:S(2)}) copy-start(bf16[1,4096,128]{2,1,0:T(8,128)(2,1)} %param.14) | copy-start | bytes 3145732
  0.6 13.5 %copy-start = (f32[128,128]{1,0:T(8,128)S(1)}, f32[128,128]{1,0:T(8,128)}, u32[]{:S(2)}) copy-start(f32[128,128]{1,0:T(8,128)} %param.15) | copy-start | bytes 196612
  2.9 11.3 %collective-permute-start.9 = (f32[16,128,128]{2,1,0:T(8,128)}, f32[16,128,128]{2,1,0:T(8,128)S(1)}, u32[]{:S(2)}, u32[]{:S(2)}) collective-permute-start(f32[16,128,128]{2,1,0:T(8,128)} %bitcast_convert_fusion.1), channel_id=1, source_target_pairs={{0,16},{16,0},{1,17},{17,1},{2,18},{18,2},{3,19},{19,3},{4,20},{20... | collective-permute-start | bytes 3145736 | tf_op jit(solution)/shard_map/ppermute | solution.py:247
  14.1 42.4 %copy-start.4 = (f32[128]{0:T(128)S(1)}, f32[128]{0:T(128)}, u32[]{:S(2)}) copy-start(f32[128]{0:T(128)} %param.17) | copy-start | bytes 1540
  14.1 56.4 %copy-start.3 = (f32[128]{0:T(128)S(1)}, f32[128]{0:T(128)}, u32[]{:S(2)}) copy-start(f32[128]{0:T(128)} %param.16) | copy-start | bytes 1540
  42.3 14.2 %collective-permute-start.8 = (f32[16,128,128]{2,1,0:T(8,128)S(1)}, f32[16,128,128]{2,1,0:T(8,128)S(1)}, u32[]{:S(2)}, u32[]{:S(2)}) collective-permute-start(f32[16,128,128]{2,1,0:T(8,128)S(1)} %bitcast.39), channel_id=1, source_target_pairs={{0,16},{16,0},{1,17},{17,1},{2,18},{18,2},{3,19},{19,3},{4,20},{20... | collective-permute-start | bytes 3145736 | tf_op jit(solution)/shard_map/cond/branch_0_fun/ppermute | solution.py:208
  56.5 14.1 %copy-start.2 = (f32[128]{0:T(128)}, f32[128]{0:T(128)S(1)}, u32[]{:S(2)}) copy-start(f32[128]{0:T(128)S(1)} %get-tuple-element.193) | copy-start | bytes 1540
  89.8 7.4 %collective-permute-start.1 = (f32[16,136,128]{2,1,0:T(8,128)S(1)}, f32[16,136,128]{2,1,0:T(8,128)S(1)}, u32[]{:S(2)}, u32[]{:S(2)}) collective-permute-start(f32[16,136,128]{2,1,0:T(8,128)S(1)} %all_to_all.96.mine), channel_id=1, source_target_pairs={{0,16},{16,0},{1,17},{17,1},{2,18},{18,2},{3,19},{19,3},{4,20},{20... | collective-permute-start | bytes 3342344 | tf_op jit(solution)/shard_map/cond/branch_0_fun/ppermute | solution.py:226
  98.1 1.3 %copy-start.5 = (f32[16,2,128,128]{3,2,1,0:T(8,128)}, f32[16,2,128,128]{3,2,1,0:T(8,128)S(1)}, u32[]{:S(2)}) copy-start(f32[16,2,128,128]{3,2,1,0:T(8,128)S(1)} %get-tuple-element.169) | copy-start | bytes 6291460
